TPU v7x, 128 devices: a whole 4x4x4 slice. The times are simulated.
128 devices in a mesh: dp: 8 (over z, y_hi), tensor: 16 (over x, y_lo, core).
Axes of the slice: x: 4, y: 4 (y_hi: 2, y_lo: 2; y = y_hi * 2 + y_lo), z: 4, core: 2. Of those that a mesh axis runs over, the one named last changes fastest.
Arguments:
- grad: float32 [8192, 8192], P('tensor', 'dp')
- owner_order: int32 [8, 32], P('dp'), may hold values from 0 to 31, each once within a row
- left_stat: float32 [256, 512, 512], P(('dp', 'tensor'))
- right_stat: float32 [256, 512, 512], P(('dp', 'tensor'))
- left_root: bfloat16 [256, 512, 512], P(('dp', 'tensor'))
- right_root: bfloat16 [256, 512, 512], P(('dp', 'tensor'))
- momentum: float32 [256, 512, 512], P(('dp', 'tensor')), may hold values from -6 to 6
- second: float32 [256, 512, 512], P(('dp', 'tensor')), may hold values from 0.25 to 4
Outputs:
- new_left: float32 [256, 512, 512], P(('dp', 'tensor'))
- new_right: float32 [256, 512, 512], P(('dp', 'tensor'))
- new_momentum: float32 [256, 512, 512], P(('dp', 'tensor'))
- new_second: float32 [256, 512, 512], P(('dp', 'tensor'))
- update: float32 [8192, 8192], P('tensor', 'dp')
Inputs may be any that keep to these rules, and one draw needn't show every extreme that they name: `owner_order`: each row lists every block number of 0 to 31 once.
All inputs are finite; a program needn't handle non-finite values.
Results may differ from a plain program's by a relative error of at most 0.004.
Values sent between devices are 32-bit elements; how exact they have to be, the bound alone decides.
No kernel may reach another device: no remote copies, remote signals or barrier semaphores. Data moves between devices by JAX's collectives and lax.ppermute only.
A program may use at most 128 MiB of HBM per device.

v0:
```python
import jax
import jax.numpy as jnp
from jax import lax
from jax.sharding import PartitionSpec as P


def body(grad, owner_order, left_stat, right_stat, left_root, right_root, momentum, second):
    row_count, col_width = grad.shape
    slot_count, block_size = (left_stat.shape[0], left_stat.shape[1])
    peer_count = lax.axis_size("tensor")
    piece_rows = block_size // peer_count
    row_groups = row_count // piece_rows
    col_blocks = col_width // block_size
    group_count = row_groups * col_blocks
    order_row = owner_order[0]
    send_order = order_row.reshape(peer_count, slot_count).T.reshape(group_count)
    pieces = grad.reshape(row_groups, piece_rows, col_blocks, block_size).transpose(0, 2, 1, 3)
    pieces = pieces.reshape(group_count, piece_rows, block_size)
    outgoing = jnp.take(pieces, send_order, axis=0).reshape(
        slot_count, peer_count, piece_rows, block_size
    )
    arrived = lax.all_to_all(outgoing, "tensor", split_axis=1, concat_axis=1, tiled=True)
    held = arrived.reshape(slot_count, block_size, block_size)
    gram_left = jnp.einsum(
        "sij,skj->sik",
        held,
        held,
        precision=lax.Precision.HIGHEST,
        preferred_element_type=jnp.float32,
    )
    gram_right = jnp.einsum(
        "sji,sjk->sik",
        held,
        held,
        precision=lax.Precision.HIGHEST,
        preferred_element_type=jnp.float32,
    )
    new_left = 0.9 * left_stat + 0.1 / block_size * gram_left
    new_right = 0.9 * right_stat + 0.1 / block_size * gram_right
    low_grad = held.astype(jnp.bfloat16)
    left_applied = jnp.einsum(
        "sij,sjk->sik", left_root, low_grad, preferred_element_type=jnp.float32
    ).astype(jnp.bfloat16)
    shampoo = jnp.einsum(
        "sij,sjk->sik", left_applied, right_root, preferred_element_type=jnp.float32
    )
    new_second = 0.99 * second + 0.01 * held * held
    adam = held / (jnp.sqrt(new_second) + 1e-08)
    adam_sq, shampoo_sq = lax.psum(
        (jnp.sum(adam * adam), jnp.sum(shampoo * shampoo)), ("dp", "tensor")
    )
    graft_scale = jnp.sqrt(adam_sq) / (jnp.sqrt(shampoo_sq) + 1e-06)
    new_momentum = 0.9 * momentum + graft_scale * shampoo
    flat_ids = jnp.arange(group_count, dtype=jnp.int32)
    inverse = jnp.sum(
        flat_ids[:, None] * (send_order[:, None] == flat_ids[None, :]).astype(jnp.int32), axis=0
    )
    step_blocks = -(0.9 * new_momentum + graft_scale * shampoo)
    returned = lax.all_to_all(
        step_blocks.reshape(slot_count, peer_count, piece_rows, block_size),
        "tensor",
        split_axis=1,
        concat_axis=1,
        tiled=True,
    )
    flat_pieces = returned.reshape(group_count, piece_rows, block_size)
    ordered = jnp.take(flat_pieces, inverse, axis=0).reshape(
        row_groups, col_blocks, piece_rows, block_size
    )
    update = ordered.transpose(0, 2, 1, 3).reshape(row_count, col_width)
    return (new_left, new_right, new_momentum, new_second, update)


def solution(mesh):
    placed = (
        P("tensor", "dp"),
        P("dp", None),
        P(("dp", "tensor"), None, None),
        P(("dp", "tensor"), None, None),
        P(("dp", "tensor"), None, None),
        P(("dp", "tensor"), None, None),
        P(("dp", "tensor"), None, None),
        P(("dp", "tensor"), None, None),
    )
    return jax.shard_map(
        body,
        mesh=mesh,
        in_specs=placed,
        out_specs=(
            P(("dp", "tensor"), None, None),
            P(("dp", "tensor"), None, None),
            P(("dp", "tensor"), None, None),
            P(("dp", "tensor"), None, None),
            P("tensor", "dp"),
        ),
        check_vma=False,
    )
```

profile of v0, /device:TPU:9, one launch (start us, length us, event | category | flops | bytes accessed | tf_op | source)
XLA Modules:
  0.0 168.0 jit_solution(2107099826161752788)
XLA Ops:
  0.6 0.0 copy-start
  0.6 0.5 broadcast.33
  1.2 1.3 reduce.3
  2.5 0.1 reshape_squeeze.3
  2.6 0.1 copy.42
  2.6 0.1 reshape.45
  2.8 3.0 %reshape.43 = f32[16,32,2,512]{3,2,1,0:T(2,128)S(1)} reshape(f32[512,1024]{1,0:T(8,128)} %param.10) | data formatting | bytes 4194304 | tf_op jit(solution)/shard_map/reshape | solution.py:17
  5.8 1.7 %copy.43 = f32[16,2,32,512]{3,2,1,0:T(8,128)} copy(f32[16,2,32,512]{3,1,2,0:T(2,128)S(1)} %bitcast.30) | data formatting | bytes 4194304 | tf_op jit(solution)/shard_map/transpose | solution.py:17
  7.5 2.3 %gather_fusion = f32[32,32,512]{2,1,0:T(8,128)S(1)} fusion(f32[32,32,512]{2,1,0:T(8,128)} %bitcast.25, s32[1024]{0:T(1024)S(1)} %pad_clamp_fusion.1), kind=kCustom, calls=%fused_computation.clone | custom fusion | bytes 4194432 | tf_op jit(solution)/shard_map/jit(_take)/gather | solution.py:19
  9.8 0.2 broadcast_select_fusion.1
  10.0 0.3 copy.44
  10.3 32.2 %all_to_all.10 = f32[2,16,32,512]{3,2,0,1:T(8,128)S(1)} all-to-all(f32[2,16,32,512]{3,2,0,1:T(8,128)S(1)} %copy.44), channel_id=1, replica_groups=mesh['dp'=8,'tensor'=16] {'tensor'}, dimensions={1} | all-to-all | bytes 4194304 | tf_op jit(solution)/shard_map/all_to_all | solution.py:22
  42.5 0.0 copy-start.1
  42.5 0.2 copy.45
  42.7 1.3 copy-done.1
  44.1 3.0 %multiply_reduce_fusion.1 = (f32[]{:T(128)}, f32[2,512,512]{2,1,0:T(8,128)}) fusion(f32[2,16,32,512]{3,2,1,0:T(8,128)S(1)} %copy.45, f32[2,512,512]{2,1,0:T(8,128)S(1)} %copy-done.1), kind=kLoop, calls=%fused_computation.6 | loop fusion | flops 4194303 | bytes 6291460 | tf_op jit(solution)/shard_map/reduce_sum | solution.py:50
  47.1 0.0 copy-done
  47.1 4.6 %multiply_reduce_fusion = (f32[]{:T(128)}, f32[2,512,512]{2,1,0:T(8,128)}) fusion(bf16[2,512,512]{2,1,0:T(8,128)(2,1)S(1)} %copy-done, bf16[2,512,512]{2,1,0:T(8,128)(2,1)} %param.14, f32[2,512,512]{2,1,0:T(8,128)S(1)} %bitcast.22), kind=kOutput, calls=%fused_computation.5 | convolution fusion | flops 1075838976 | bytes 6291460 | tf_op jit(solution)/shard_map/sij,sjk->sik/dot_general | solution.py:44
  51.7 65.5 %all-reduce = (f32[]{:T(128)}, f32[]{:T(128)}) all-reduce(f32[]{:T(128)} %get-tuple-element.10, f32[]{:T(128)} %get-tuple-element.12), channel_id=1, replica_groups=mesh['dp'=8,'tensor'=16] {'dp','tensor'}, use_global_device_ids=true, to_apply=%region_1.3 | all-reduce | flops 2 | bytes 16 | tf_op jit(solution)/shard_map/psum | solution.py:49
  118.6 4.4 %add_negate_fusion = (f32[2,512,512]{2,1,0:T(8,128)S(1)}, f32[2,512,512]{2,1,0:T(8,128)}) fusion(f32[2,512,512]{2,1,0:T(8,128)} %get-tuple-element.13, f32[]{:T(128)S(6)} %div.7, f32[2,512,512]{2,1,0:T(8,128)} %param.16), kind=kLoop, calls=%fused_computation.4 | loop fusion | flops 3145728 | bytes 8388612 | tf_op jit(solution)/shard_map/neg | solution.py:58
  123.0 1.5 copy.49
  124.5 5.7 %all-to-all-start.1 = ((f32[2,16,32,512]{3,2,0,1:T(8,128)}), f32[2,16,32,512]{3,2,0,1:T(8,128)}, u32[]{:S(2)}, u32[]{:S(2)}) async-start(f32[2,16,32,512]{3,2,0,1:T(8,128)} %copy.49), calls=%async_computation.1 | async-start | bytes 4194304 | tf_op jit(solution)/shard_map/all_to_all | solution.py:59
  130.2 0.1 select_reduce_fusion
  130.3 0.0 copy-start.2
  130.3 6.1 %multiply_add_fusion.1 = f32[2,512,512]{2,1,0:T(8,128)} fusion(f32[2,512,512]{2,1,0:T(8,128)} %param.13, f32[2,512,512]{2,1,0:T(8,128)S(1)} %bitcast.23), kind=kOutput, calls=%fused_computation.8 | convolution fusion | flops 3222798336 | bytes 6291456 | tf_op jit(solution)/shard_map/sji,sjk->sik/dot_general | solution.py:31
  136.4 0.0 copy-done.2
  136.4 5.0 %multiply_add_fusion.2 = f32[2,512,512]{2,1,0:T(8,128)} fusion(f32[2,512,512]{2,1,0:T(8,128)S(1)} %copy-done.2, f32[2,512,512]{2,1,0:T(8,128)S(1)} %bitcast.24), kind=kOutput, calls=%fused_computation.9 | convolution fusion | flops 3222798336 | bytes 6291456 | tf_op jit(solution)/shard_map/sij,skj->sik/dot_general | solution.py:24
  141.4 17.5 %all-to-all-done.1 = f32[2,16,32,512]{3,2,0,1:T(8,128)} async-done(((f32[2,16,32,512]{3,2,0,1:T(8,128)}), f32[2,16,32,512]{3,2,0,1:T(8,128)}, u32[]{:S(2)}, u32[]{:S(2)}) %all-to-all-start.1) | async-done | bytes 2097184 | tf_op jit(solution)/shard_map/all_to_all | solution.py:59
  158.9 3.2 %copy.50 = f32[2,16,32,512]{3,2,1,0:T(8,128)} copy(f32[2,16,32,512]{3,2,0,1:T(8,128)} %all-to-all-done.1) | data formatting | bytes 4194304 | tf_op jit(solution)/shard_map/all_to_all | solution.py:59
  162.1 2.3 %gather_fusion.1 = f32[32,32,512]{2,1,0:T(8,128)S(1)} fusion(f32[32,32,512]{2,1,0:T(8,128)} %bitcast.27, s32[1024]{0:T(1024)S(1)} %pad_clamp_fusion), kind=kCustom, calls=%fused_computation.1.clone | custom fusion | bytes 4194432 | tf_op jit(solution)/shard_map/jit(_take)/gather | solution.py:67
  164.4 0.2 broadcast_select_fusion
  164.6 1.6 copy.51
  166.3 1.8 %copy.55 = f32[64,8,2,512]{3,1,2,0:T(8,128)} copy(f32[64,8,2,512]{3,2,1,0:T(2,128)S(1)} %bitcast.29) | data formatting | bytes 4194304
  (6 shorter events, 0.0 us)
Async XLA Ops:
  0.6 46.4 %copy-start = (bf16[2,512,512]{2,1,0:T(8,128)(2,1)S(1)}, bf16[2,512,512]{2,1,0:T(8,128)(2,1)}, u32[]{:S(2)}) copy-start(bf16[2,512,512]{2,1,0:T(8,128)(2,1)} %param.15) | copy-start | bytes 3145732
  42.5 1.6 copy-start.1
  124.5 34.4 %all-to-all-start.1 = ((f32[2,16,32,512]{3,2,0,1:T(8,128)}), f32[2,16,32,512]{3,2,0,1:T(8,128)}, u32[]{:S(2)}, u32[]{:S(2)}) async-start(f32[2,16,32,512]{3,2,0,1:T(8,128)} %copy.49), calls=%async_computation.1 | async-start | bytes 4194304 | tf_op jit(solution)/shard_map/all_to_all | solution.py:59
  130.3 6.2 %copy-start.2 = (f32[2,512,512]{2,1,0:T(8,128)S(1)}, f32[2,512,512]{2,1,0:T(8,128)}, u32[]{:S(2)}) copy-start(f32[2,512,512]{2,1,0:T(8,128)} %param.12) | copy-start | bytes 6291460
where the time goes:
time: 169 us; the launch traced here: 168 us
  blocking collectives  97.7 us (58%)
  local copies, waits for them, and re-layouts  20 us (12%)
  waiting for transfers between devices  17.5 us (10%)
  matrix products  15.7 us (9%)
  other arithmetic  9.22 us (5%)
  starting transfers between devices  5.67 us (3%)
  between operations  2.17 us (1%)
    psum x1, blocking collectives, body(): lax.psum((jnp.sum(adam * adam), jnp.sum(shampoo * shampoo)), ('dp', 'tens...  65.5 us
    all_to_all x1, blocking collectives, body(): lax.all_to_all(outgoing, 'tensor', split_axis=1, concat_axis=1, tiled=True)  32.2 us
    all_to_all x1, waiting for transfers between devices, body(): lax.all_to_all(step_blocks.reshape(slot_count, peer_count, piece_rows, bl...  17.5 us
    dot_general x1, matrix products, body(): jnp.einsum('sji,sjk->sik', held, held, precision=lax.Precision.HIGHEST, p...  6.14 us
    all_to_all x1, starting transfers between devices, body(): lax.all_to_all(step_blocks.reshape(slot_count, peer_count, piece_rows, bl...  5.67 us
    dot_general x1, matrix products, body(): jnp.einsum('sij,skj->sik', held, held, precision=lax.Precision.HIGHEST, p...  4.99 us
    dot_general x1, matrix products, body(): jnp.einsum('sij,sjk->sik', left_applied, right_root, preferred_element_ty...  4.6 us
    neg x1, other arithmetic, body(): step_blocks = -(0.9 * new_momentum + graft_scale * shampoo)  4.36 us
  transfers between devices with their start and end apart: 1, of which 1 were waited for; matrix products, arithmetic and copies ran while one was open for 7% of the time, Pallas kernels for 0%

commit v1 on v0

v1 whole, which is shorter than its diff:
```python
import functools

import jax
import jax.numpy as jnp
from jax import lax
from jax.experimental import pallas as pl
from jax.experimental.pallas import tpu as pltpu
from jax.sharding import PartitionSpec as P

ANY = pl.BlockSpec(memory_space=pl.ANY)
VMEM = pl.BlockSpec(memory_space=pltpu.VMEM)
DMA = pltpu.SemaphoreType.DMA
MIB = 1 << 20
F32 = jnp.float32
BF16 = jnp.bfloat16
CHUNKS = 4


def in_vmem(x):
    return pltpu.with_memory_space_constraint(x, pltpu.VMEM)


def in_hbm(x):
    return pltpu.with_memory_space_constraint(x, pltpu.HBM)


def params(mib):
    return pltpu.CompilerParams(vmem_limit_bytes=mib * MIB)


def copy(source, target, sem):
    return pltpu.make_async_copy(source, target, sem)


def started(source, target, sem):
    moved = copy(source, target, sem)
    moved.start()
    return moved


def wait_all(ref, sem):
    copy(ref, ref, sem).wait()


def piece_of(ref, block, piece_rows, block_size):
    col_blocks = ref.shape[1] // block_size
    row = pl.multiple_of((block // col_blocks) * piece_rows, piece_rows)
    col = pl.multiple_of((block % col_blocks) * block_size, block_size)
    return ref.at[pl.ds(row, piece_rows), pl.ds(col, block_size)]


def rows_of(peer, piece_rows):
    return slice(peer * piece_rows, (peer + 1) * piece_rows)


def pack_kernel(order_ref, grad_ref, out_ref, sem):
    peers, slots, piece_rows, block_size = out_ref.shape
    for peer in range(peers):
        for slot in range(slots):
            block = order_ref[0, peer * slots + slot]
            started(
                piece_of(grad_ref, block, piece_rows, block_size), out_ref.at[peer, slot], sem
            )
    wait_all(out_ref, sem)


def unpack_kernel(order_ref, moved_ref, out_ref, sem):
    peers, slots, piece_rows, block_size = moved_ref.shape
    for peer in range(peers):
        for slot in range(slots):
            block = order_ref[0, peer * slots + slot]
            started(
                moved_ref.at[peer, slot], piece_of(out_ref, block, piece_rows, block_size), sem
            )
    wait_all(moved_ref, sem)


def sum_rows(x):
    return jnp.sum(x.reshape(-1, 8, x.shape[-1]), axis=0)


def mid_kernel(
    arrived_ref, second_ref, left_ref, right_ref, shampoo_ref, held_ref, sums_ref, low_ref, sem
):
    peers, slots, piece_rows, block_size = arrived_ref.shape
    half = block_size // 2
    half_peers = peers // 2
    kept = started(arrived_ref, held_ref, sem)
    adam_sq = jnp.zeros((8, block_size), F32)
    shampoo_sq = jnp.zeros((8, block_size), F32)
    for slot in range(slots):
        for peer in range(peers):
            rows = rows_of(peer, piece_rows)
            held = arrived_ref[peer, slot]
            low_ref[slot, rows, :] = held.astype(BF16)
            new_second = 0.99 * second_ref[slot, rows, :] + 0.01 * held * held
            adam = held / (jnp.sqrt(new_second) + 1e-08)
            adam_sq += sum_rows(adam * adam)
    for slot in range(slots):
        for part in range(2):
            rows = slice(part * half, (part + 1) * half)
            left_applied = jnp.dot(
                left_ref[slot, rows, :], low_ref[slot], preferred_element_type=F32
            ).astype(BF16)
            shampoo = jnp.dot(left_applied, right_ref[slot], preferred_element_type=F32)
            shampoo_ref[part * half_peers : (part + 1) * half_peers, slot] = shampoo.reshape(
                half_peers, piece_rows, block_size
            )
            shampoo_sq += sum_rows(shampoo * shampoo)
    ranks = sums_ref.shape[0]
    sums_ref[:, 0, :] = jnp.full((ranks, 128), jnp.sum(adam_sq), F32)
    sums_ref[:, 1, :] = jnp.full((ranks, 128), jnp.sum(shampoo_sq), F32)
    kept.wait()


def graft_of(sums_ref):
    root = jnp.sqrt(jnp.sum(sums_ref[...], axis=0))
    return root[0:1, 0:1] / (root[1:2, 0:1] + 1e-06)


def gram_kernel(
    held_ref, second_ref, left_ref, right_ref,
    new_left_ref, new_right_ref, new_second_ref,
    held_here, second_here, left_here, right_here, high_ref, low_ref, sems, store_sem,
):
    peers, slots, piece_rows, block_size = held_ref.shape
    loads = [
        [
            started(source.at[(*at, slot)], target.at[(*at, slot)], sems.at[slot, k])
            for k, (source, target, at) in enumerate(
                (
                    (held_ref, held_here, (slice(None),)),
                    (left_ref, left_here, ()),
                    (right_ref, right_here, ()),
                    (second_ref, second_here, ()),
                )
            )
        ]
        for slot in range(slots)
    ]
    scale = 0.1 / block_size
    half = block_size // 2
    for slot in range(slots):
        loads[slot][0].wait()
        for peer in range(peers):
            rows = rows_of(peer, piece_rows)
            held = held_here[peer, slot]
            high = held.astype(BF16)
            high_ref[slot, rows, :] = high
            low_ref[slot, rows, :] = (held - high.astype(F32)).astype(BF16)
        for k, (here, ref) in enumerate(
            ((left_here, new_left_ref), (right_here, new_right_ref))
        ):
            product = functools.partial(
                lax.dot_general,
                dimension_numbers=(((1 - k,), (1 - k,)), ((), ())),
                preferred_element_type=F32,
            )
            loads[slot][1 + k].wait()
            for part in range(2):
                cut = slice(part * half, (part + 1) * half)
                at = (slot, cut, slice(None)) if k == 0 else (slot, slice(None), cut)
                gram = (
                    product(high_ref[at], low_ref[slot])
                    + product(low_ref[at], high_ref[slot])
                    + product(high_ref[at], high_ref[slot])
                )
                here[slot, cut, :] = 0.9 * here[slot, cut, :] + scale * gram
            started(here.at[slot], ref.at[slot], store_sem)
        loads[slot][3].wait()
        for peer in range(peers):
            rows = rows_of(peer, piece_rows)
            held = held_here[peer, slot]
            second_here[slot, rows, :] = 0.99 * second_here[slot, rows, :] + 0.01 * held * held
        started(second_here.at[slot], new_second_ref.at[slot], store_sem)
    for here in (left_here, right_here, second_here):
        wait_all(here, store_sem)


def step_kernel(
    sums_ref, shampoo_ref, momentum_ref, _, step_ref, new_momentum_ref, here_ref, sems, store_sem
):
    peers, slots, piece_rows, block_size = shampoo_ref.shape
    count = peers // CHUNKS
    parts = [
        (slot, chunk, (slot, pl.ds(chunk * count * piece_rows, count * piece_rows)))
        for chunk in range(CHUNKS)
        for slot in range(slots)
    ]
    loads = [
        started(momentum_ref.at[at], here_ref.at[at], sems.at[slot, chunk])
        for slot, chunk, at in parts
    ]
    graft = graft_of(sums_ref)
    for load, (slot, chunk, at) in zip(loads, parts):
        load.wait()
        for peer in range(chunk * count, (chunk + 1) * count):
            rows = rows_of(peer, piece_rows)
            scaled = graft * shampoo_ref[peer, slot]
            new_momentum = 0.9 * here_ref[slot, rows, :] + scaled
            here_ref[slot, rows, :] = new_momentum
            step_ref[peer, slot] = -(0.9 * new_momentum + scaled)
        started(here_ref.at[at], new_momentum_ref.at[at], store_sem)
    wait_all(here_ref, store_sem)


def body(grad, owner_order, left_stat, right_stat, left_root, right_root, momentum, second):
    slots, block_size = left_stat.shape[0], left_stat.shape[1]
    peers = lax.axis_size("tensor")
    ranks = peers * lax.axis_size("dp")
    piece_rows = block_size // peers
    pair = (peers, slots, piece_rows, block_size)
    blocks = (slots, block_size, block_size)
    hbm = lambda shape: pltpu.HBM(shape, F32)
    vmem = lambda shape, dtype=F32: pltpu.VMEM(shape, dtype)
    over_tensor = functools.partial(
        lax.all_to_all, axis_name="tensor", split_axis=0, concat_axis=0, tiled=True
    )
    order = in_hbm(owner_order)

    outgoing = pl.pallas_call(
        pack_kernel,
        out_shape=jax.ShapeDtypeStruct(pair, F32),
        grid_spec=pltpu.PrefetchScalarGridSpec(
            num_scalar_prefetch=1, grid=(1,), in_specs=[ANY], out_specs=ANY,
            scratch_shapes=[DMA],
        ),
        compiler_params=params(2),
        name="pack",
    )(order, in_hbm(grad))
    arrived = over_tensor(outgoing)

    shampoo, held, sums = pl.pallas_call(
        mid_kernel,
        out_shape=(vmem(pair), hbm(pair), hbm((ranks, 2, 128))),
        in_specs=[VMEM] * 4,
        out_specs=(VMEM, ANY, VMEM),
        scratch_shapes=[vmem(blocks, BF16), DMA],
        compiler_params=params(16),
        name="mid",
    )(in_vmem(arrived), in_vmem(second), in_vmem(left_root), in_vmem(right_root))
    sums = lax.all_to_all(
        sums, ("dp", "tensor"), split_axis=0, concat_axis=0, tiled=True
    )

    new_left, new_right, new_second = pl.pallas_call(
        gram_kernel,
        out_shape=(hbm(blocks),) * 3,
        in_specs=[ANY] * 4,
        out_specs=(ANY,) * 3,
        scratch_shapes=[vmem(pair)] + [vmem(blocks)] * 3 + [vmem(blocks, BF16)] * 2
        + [DMA((slots, 4)), DMA],
        compiler_params=params(24),
        cost_estimate=pl.CostEstimate(
            flops=slots * 12 * block_size**3, bytes_accessed=14 * MIB, transcendentals=0
        ),
        name="gram",
    )(in_hbm(held), in_hbm(second), in_hbm(left_stat), in_hbm(right_stat))

    step, new_momentum = pl.pallas_call(
        step_kernel,
        out_shape=(vmem(pair), hbm(blocks)),
        in_specs=[VMEM, VMEM, ANY, ANY],
        out_specs=(VMEM, ANY),
        scratch_shapes=[vmem(blocks), DMA((slots, CHUNKS)), DMA],
        compiler_params=params(8),
        name="step",
    )(sums, in_vmem(shampoo), in_hbm(momentum), in_hbm(new_second))
    returned = over_tensor(step)

    update = pl.pallas_call(
        unpack_kernel,
        out_shape=hbm(grad.shape),
        grid_spec=pltpu.PrefetchScalarGridSpec(
            num_scalar_prefetch=1, grid=(1,), in_specs=[ANY], out_specs=ANY,
            scratch_shapes=[DMA],
        ),
        compiler_params=params(2),
        name="unpack",
    )(order, in_vmem(returned))
    return (new_left, new_right, new_momentum, new_second, update)


def solution(mesh):
    owned = P(("dp", "tensor"), None, None)
    return jax.shard_map(
        body,
        mesh=mesh,
        in_specs=(P("tensor", "dp"), P("dp", None)) + (owned,) * 6,
        out_specs=(owned,) * 4 + (P("tensor", "dp"),),
        check_vma=False,
    )
```

time: 169 us -> 94.1 us (0.56)
  blocking collectives: 97.7 us -> 62.7 us
  local copies, waits for them, and re-layouts: 20 us -> 1.34 us
  Pallas kernels: 0 us -> 17.3 us
  waiting for transfers between devices: 17.5 us -> 1.66 us
  matrix products: 15.7 us -> 0 us
  other arithmetic: 9.22 us -> 0 us
  starting transfers between devices: 5.67 us -> 9.19 us
    psum x1 -> x0, blocking collectives: 65.5 us -> none  [body(): lax.psum((jnp.sum(adam * adam), jnp.sum(shampoo * shampoo)), ('dp', 'tens...]
    all_to_all x1 -> x2, blocking collectives: 32.2 us -> 62.7 us  [the longest x1 32.5 us: body(): arrived = over_tensor(outgoing)]
    pallas_call x0 -> x5, Pallas kernels: none -> 17.3 us  [the longest x1 7.45 us: body(): pl.pallas_call(gram_kernel, out_shape=(hbm(blocks),) * 3, in_specs=[ANY]...]
    all_to_all x1, waiting for transfers between devices: 17.5 us -> 1.66 us  [body(): lax.all_to_all(sums, ('dp', 'tensor'), split_axis=0, concat_axis=0, tiled...]
    dot_general x3 -> x0, matrix products: 15.7 us -> none  [the longest x1 6.14 us: body(): jnp.einsum('sji,sjk->sik', held, held, precision=lax.Precision.HIGHEST, p...]
    reshape x4 -> x0, local copies, waits for them, and re-layouts: 4.92 us -> none  [the longest x1 3.03 us: body(): grad.reshape(row_groups, piece_rows, col_blocks, block_size)]
    gather x2 -> x0, local copies, waits for them, and re-layouts: 4.54 us -> none  [the longest x1 2.27 us: body(): jnp.take(pieces, send_order, axis=0)]
    neg x1 -> x0, other arithmetic: 4.36 us -> none  [body(): step_blocks = -(0.9 * new_momentum + graft_scale * shampoo)]
  transfers between devices with their start and end apart: 1 -> 1, of which waited for: 1 -> 1; matrix products, arithmetic and copies ran while one was open for 7% -> 0% of each run, Pallas kernels for 0% -> 8%
where the time goes in v1:
time: 94.1 us; the launch traced here: 92.9 us
  blocking collectives  62.7 us (67%)
  Pallas kernels  17.3 us (18%)
  starting transfers between devices  9.19 us (10%)
  waiting for transfers between devices  1.66 us (2%)
  local copies, waits for them, and re-layouts  1.34 us (1%)
    all_to_all x1, blocking collectives, body(): arrived = over_tensor(outgoing)  32.5 us
    all_to_all x1, blocking collectives, body(): returned = over_tensor(step)  30.3 us
    all_to_all x1, starting transfers between devices, body(): lax.all_to_all(sums, ('dp', 'tensor'), split_axis=0, concat_axis=0, tiled...  9.19 us
    pallas_call x1, Pallas kernels, body(): pl.pallas_call(gram_kernel, out_shape=(hbm(blocks),) * 3, in_specs=[ANY]...  7.45 us
    pallas_call x1, Pallas kernels, body(): pl.pallas_call(mid_kernel, out_shape=(vmem(pair), hbm(pair), hbm((ranks,...  3.16 us
    pallas_call x1, Pallas kernels, body(): pl.pallas_call(step_kernel, out_shape=(vmem(pair), hbm(blocks)), in_specs...  2.39 us
    pallas_call x1, Pallas kernels, body(): pl.pallas_call(pack_kernel, out_shape=jax.ShapeDtypeStruct(pair, F32), gr...  2.28 us
    pallas_call x1, Pallas kernels, body(): pl.pallas_call(unpack_kernel, out_shape=hbm(grad.shape), grid_spec=pltpu....  1.96 us
  transfers between devices with their start and end apart: 1, of which 1 were waited for; matrix products, arithmetic and copies ran while one was open for 0% of the time, Pallas kernels for 8%

profile of v1, /device:TPU:9, one launch (start us, length us, event | category | flops | bytes accessed | tf_op | source)
XLA Modules:
  0.0 92.9 jit_solution(4646093995271830078)
XLA Ops:
  0.6 2.3 %pack.1 = f32[16,2,32,512]{3,2,1,0:T(8,128)S(1)} custom-call(s32[1,32]{1,0:T(1,128)} %order_ref.3, f32[512,1024]{1,0:T(8,128)} %grad_ref.1), custom_call_target="tpu_custom_call" | custom-call | tf_op jit(solution)/shard_map/pack/pallas_call | solution.py:221
  2.9 0.0 copy-start
  2.9 0.0 copy-start.3
  2.9 0.0 copy-start.4
  3.0 32.5 %all_to_all.15.arrived_ref = f32[16,2,32,512]{3,2,1,0:T(8,128)S(1)} all-to-all(f32[16,2,32,512]{3,2,1,0:T(8,128)S(1)} %pack.1), channel_id=1, replica_groups=mesh['dp'=8,'tensor'=16] {'tensor'}, dimensions={0} | all-to-all | bytes 4194304 | tf_op jit(solution)/shard_map/all_to_all | solution.py:231
  35.4 0.0 copy-done
  35.4 0.0 copy-done.3
  35.4 0.0 copy-done.4
  35.4 3.2 %mid.1 = (f32[16,2,32,512]{3,2,1,0:T(8,128)S(1)}, f32[16,2,32,512]{3,2,1,0:T(8,128)}, f32[128,2,128]{2,1,0:T(2,128)}) custom-call(f32[16,2,32,512]{3,2,1,0:T(8,128)S(1)} %all_to_all.15.arrived_ref, f32[2,512,512]{2,1,0:T(8,128)S(1)} %copy-done, bf16[2,512,512]{2,1,0:T(8,128)(2,1)S(1)} %copy-done.3, bf16[2,512,512]{2,1,0:T(8,128)(2,1)S(1)} %copy-done.4), custom_call_target="tpu_custom_call" | custom-call | tf_op jit(solution)/shard_map/mid/pallas_call | solution.py:233
  38.6 0.0 copy-start.1
  38.6 1.3 %copy-done.1 = f32[16,2,32,512]{3,2,1,0:T(8,128)} copy-done((f32[16,2,32,512]{3,2,1,0:T(8,128)}, f32[16,2,32,512]{3,2,1,0:T(8,128)S(1)}, u32[]{:S(2)}) %copy-start.1) | copy-done | bytes 2097176
  39.9 9.2 %all-to-all-start.1 = ((f32[128,2,128]{2,1,0:T(2,128)}), f32[128,2,128]{2,1,0:T(2,128)S(1)}, u32[]{:S(2)}, u32[]{:S(2)}) async-start(f32[128,2,128]{2,1,0:T(2,128)} %get-tuple-element.16), calls=%async_computation.1 | async-start | bytes 262144 | tf_op jit(solution)/shard_map/all_to_all | solution.py:242
  49.1 0.0 copy-start.2
  49.1 7.5 %gram.1 = (f32[2,512,512]{2,1,0:T(8,128)}, f32[2,512,512]{2,1,0:T(8,128)}, f32[2,512,512]{2,1,0:T(8,128)}) custom-call(f32[16,2,32,512]{3,2,1,0:T(8,128)} %get-tuple-element.13.held_ref, f32[2,512,512]{2,1,0:T(8,128)} %second_ref.3, f32[2,512,512]{2,1,0:T(8,128)} %left_ref.3, f32[2,512,512]{2,1,0:T(8,128)} %right_ref.3), custom_call_target="tpu_custom_call" | custom-call | flops 3221225472 | bytes 14680064 | tf_op jit(solution)/shard_map/gram/pallas_call | solution.py:246
  56.6 1.7 %all-to-all-done.1.sums_ref = f32[128,2,128]{2,1,0:T(2,128)S(1)} async-done(((f32[128,2,128]{2,1,0:T(2,128)}), f32[128,2,128]{2,1,0:T(2,128)S(1)}, u32[]{:S(2)}, u32[]{:S(2)}) %all-to-all-start.1) | async-done | bytes 131104 | tf_op jit(solution)/shard_map/all_to_all | solution.py:242
  58.2 0.0 copy-done.2
  58.2 2.4 %step.1 = (f32[16,2,32,512]{3,2,1,0:T(8,128)S(1)}, f32[2,512,512]{2,1,0:T(8,128)}) custom-call(f32[128,2,128]{2,1,0:T(2,128)S(1)} %all-to-all-done.1.sums_ref, f32[16,2,32,512]{3,2,1,0:T(8,128)S(1)} %copy-done.2, f32[2,512,512]{2,1,0:T(8,128)} %momentum_ref.1, f32[2,512,512]{2,1,0:T(8,128)} %get-tuple-element.11._), custom_call_target="tpu_custom_call" | custom-call | tf_op jit(solution)/shard_map/step/pallas_call | solution.py:260
  60.6 30.3 %all_to_all.16.moved_ref = f32[16,2,32,512]{3,2,1,0:T(8,128)S(1)} all-to-all(f32[16,2,32,512]{3,2,1,0:T(8,128)S(1)} %get-tuple-element.20), channel_id=1, replica_groups=mesh['dp'=8,'tensor'=16] {'tensor'}, dimensions={0} | all-to-all | bytes 4194304 | tf_op jit(solution)/shard_map/all_to_all | solution.py:269
  90.9 2.0 %unpack.1 = f32[512,1024]{1,0:T(8,128)} custom-call(s32[1,32]{1,0:T(1,128)} %order_ref.3, f32[16,2,32,512]{3,2,1,0:T(8,128)S(1)} %all_to_all.16.moved_ref), custom_call_target="tpu_custom_call" | custom-call | tf_op jit(solution)/shard_map/unpack/pallas_call | solution.py:271
Async XLA Ops:
  2.9 32.5 %copy-start = (f32[2,512,512]{2,1,0:T(8,128)S(1)}, f32[2,512,512]{2,1,0:T(8,128)}, u32[]{:S(2)}) copy-start(f32[2,512,512]{2,1,0:T(8,128)} %second_ref.3) | copy-start | bytes 6291460
  2.9 32.5 %copy-start.3 = (bf16[2,512,512]{2,1,0:T(8,128)(2,1)S(1)}, bf16[2,512,512]{2,1,0:T(8,128)(2,1)}, u32[]{:S(2)}) copy-start(bf16[2,512,512]{2,1,0:T(8,128)(2,1)} %left_ref.2) | copy-start | bytes 3145732
  2.9 32.5 %copy-start.4 = (bf16[2,512,512]{2,1,0:T(8,128)(2,1)S(1)}, bf16[2,512,512]{2,1,0:T(8,128)(2,1)}, u32[]{:S(2)}) copy-start(bf16[2,512,512]{2,1,0:T(8,128)(2,1)} %right_ref.2) | copy-start | bytes 3145732
  38.6 1.3 %copy-start.1 = (f32[16,2,32,512]{3,2,1,0:T(8,128)}, f32[16,2,32,512]{3,2,1,0:T(8,128)S(1)}, u32[]{:S(2)}) copy-start(f32[16,2,32,512]{3,2,1,0:T(8,128)S(1)} %get-tuple-element.17.shampoo_ref) | copy-start | bytes 6291460
  39.9 18.3 %all-to-all-start.1 = ((f32[128,2,128]{2,1,0:T(2,128)}), f32[128,2,128]{2,1,0:T(2,128)S(1)}, u32[]{:S(2)}, u32[]{:S(2)}) async-start(f32[128,2,128]{2,1,0:T(2,128)} %get-tuple-element.16), calls=%async_computation.1 | async-start | bytes 262144 | tf_op jit(solution)/shard_map/all_to_all | solution.py:242
  49.1 9.1 %copy-start.2 = (f32[16,2,32,512]{3,2,1,0:T(8,128)S(1)}, f32[16,2,32,512]{3,2,1,0:T(8,128)}, u32[]{:S(2)}) copy-start(f32[16,2,32,512]{3,2,1,0:T(8,128)} %copy-done.1) | copy-start | bytes 6291460

commit v2 on v1

--- a/solution.py
+++ b/solution.py
@@ -80,22 +80,16 @@
 
 
 def mid_kernel(
-    arrived_ref, second_ref, left_ref, right_ref, shampoo_ref, held_ref, sums_ref, low_ref, sem
+    arrived_ref, second_ref, left_ref, right_ref, shampoo_ref, sums_ref, low_ref, here_ref, sem
 ):
     peers, slots, piece_rows, block_size = arrived_ref.shape
     half = block_size // 2
     half_peers = peers // 2
-    kept = started(arrived_ref, held_ref, sem)
     adam_sq = jnp.zeros((8, block_size), F32)
     shampoo_sq = jnp.zeros((8, block_size), F32)
     for slot in range(slots):
         for peer in range(peers):
-            rows = rows_of(peer, piece_rows)
-            held = arrived_ref[peer, slot]
-            low_ref[slot, rows, :] = held.astype(BF16)
-            new_second = 0.99 * second_ref[slot, rows, :] + 0.01 * held * held
-            adam = held / (jnp.sqrt(new_second) + 1e-08)
-            adam_sq += sum_rows(adam * adam)
+            low_ref[slot, rows_of(peer, piece_rows), :] = arrived_ref[peer, slot].astype(BF16)
     for slot in range(slots):
         for part in range(2):
             rows = slice(part * half, (part + 1) * half)
@@ -103,14 +97,22 @@
                 left_ref[slot, rows, :], low_ref[slot], preferred_element_type=F32
             ).astype(BF16)
             shampoo = jnp.dot(left_applied, right_ref[slot], preferred_element_type=F32)
-            shampoo_ref[part * half_peers : (part + 1) * half_peers, slot] = shampoo.reshape(
-                half_peers, piece_rows, block_size
-            )
+            at = (pl.ds(part * half_peers, half_peers), slot)
+            here_ref[at] = shampoo.reshape(half_peers, piece_rows, block_size)
+            started(here_ref.at[at], shampoo_ref.at[at], sem)
             shampoo_sq += sum_rows(shampoo * shampoo)
+    for slot in range(slots):
+        for peer in range(peers):
+            held = arrived_ref[peer, slot]
+            new_second = (
+                0.99 * second_ref[slot, rows_of(peer, piece_rows), :] + 0.01 * held * held
+            )
+            adam = held / (jnp.sqrt(new_second) + 1e-08)
+            adam_sq += sum_rows(adam * adam)
     ranks = sums_ref.shape[0]
     sums_ref[:, 0, :] = jnp.full((ranks, 128), jnp.sum(adam_sq), F32)
     sums_ref[:, 1, :] = jnp.full((ranks, 128), jnp.sum(shampoo_sq), F32)
-    kept.wait()
+    wait_all(here_ref, sem)
 
 
 def graft_of(sums_ref):
@@ -119,21 +121,16 @@
 
 
 def gram_kernel(
-    held_ref, second_ref, left_ref, right_ref,
+    arrived_ref, second_ref, left_ref, right_ref,
     new_left_ref, new_right_ref, new_second_ref,
-    held_here, second_here, left_here, right_here, high_ref, low_ref, sems, store_sem,
+    second_here, left_here, right_here, low_ref, sems, store_sem,
 ):
-    peers, slots, piece_rows, block_size = held_ref.shape
+    peers, slots, piece_rows, block_size = arrived_ref.shape
     loads = [
         [
-            started(source.at[(*at, slot)], target.at[(*at, slot)], sems.at[slot, k])
-            for k, (source, target, at) in enumerate(
-                (
-                    (held_ref, held_here, (slice(None),)),
-                    (left_ref, left_here, ()),
-                    (right_ref, right_here, ()),
-                    (second_ref, second_here, ()),
-                )
+            started(source.at[slot], target.at[slot], sems.at[slot, k])
+            for k, (source, target) in enumerate(
+                ((left_ref, left_here), (right_ref, right_here), (second_ref, second_here))
             )
         ]
         for slot in range(slots)
@@ -141,36 +138,26 @@
     scale = 0.1 / block_size
     half = block_size // 2
     for slot in range(slots):
-        loads[slot][0].wait()
-        for peer in range(peers):
-            rows = rows_of(peer, piece_rows)
-            held = held_here[peer, slot]
-            high = held.astype(BF16)
-            high_ref[slot, rows, :] = high
-            low_ref[slot, rows, :] = (held - high.astype(F32)).astype(BF16)
+        for peer in range(peers):
+            low_ref[slot, rows_of(peer, piece_rows), :] = arrived_ref[peer, slot].astype(BF16)
+    for slot in range(slots):
         for k, (here, ref) in enumerate(
             ((left_here, new_left_ref), (right_here, new_right_ref))
         ):
-            product = functools.partial(
-                lax.dot_general,
-                dimension_numbers=(((1 - k,), (1 - k,)), ((), ())),
-                preferred_element_type=F32,
-            )
-            loads[slot][1 + k].wait()
+            loads[slot][k].wait()
             for part in range(2):
                 cut = slice(part * half, (part + 1) * half)
                 at = (slot, cut, slice(None)) if k == 0 else (slot, slice(None), cut)
-                gram = (
-                    product(high_ref[at], low_ref[slot])
-                    + product(low_ref[at], high_ref[slot])
-                    + product(high_ref[at], high_ref[slot])
+                gram = lax.dot_general(
+                    low_ref[at], low_ref[slot], (((1 - k,), (1 - k,)), ((), ())),
+                    preferred_element_type=F32,
                 )
                 here[slot, cut, :] = 0.9 * here[slot, cut, :] + scale * gram
             started(here.at[slot], ref.at[slot], store_sem)
-        loads[slot][3].wait()
+        loads[slot][2].wait()
         for peer in range(peers):
             rows = rows_of(peer, piece_rows)
-            held = held_here[peer, slot]
+            held = arrived_ref[peer, slot]
             second_here[slot, rows, :] = 0.99 * second_here[slot, rows, :] + 0.01 * held * held
         started(second_here.at[slot], new_second_ref.at[slot], store_sem)
     for here in (left_here, right_here, second_here):
@@ -228,17 +215,17 @@
         compiler_params=params(2),
         name="pack",
     )(order, in_hbm(grad))
-    arrived = over_tensor(outgoing)
-
-    shampoo, held, sums = pl.pallas_call(
+    arrived = in_vmem(over_tensor(outgoing))
+
+    shampoo, sums = pl.pallas_call(
         mid_kernel,
-        out_shape=(vmem(pair), hbm(pair), hbm((ranks, 2, 128))),
+        out_shape=(hbm(pair), hbm((ranks, 2, 128))),
         in_specs=[VMEM] * 4,
-        out_specs=(VMEM, ANY, VMEM),
-        scratch_shapes=[vmem(blocks, BF16), DMA],
+        out_specs=(ANY, VMEM),
+        scratch_shapes=[vmem(blocks, BF16), vmem(pair), DMA],
         compiler_params=params(16),
         name="mid",
-    )(in_vmem(arrived), in_vmem(second), in_vmem(left_root), in_vmem(right_root))
+    )(arrived, in_vmem(second), in_vmem(left_root), in_vmem(right_root))
     sums = lax.all_to_all(
         sums, ("dp", "tensor"), split_axis=0, concat_axis=0, tiled=True
     )
@@ -246,16 +233,15 @@
     new_left, new_right, new_second = pl.pallas_call(
         gram_kernel,
         out_shape=(hbm(blocks),) * 3,
-        in_specs=[ANY] * 4,
+        in_specs=[VMEM] + [ANY] * 3,
         out_specs=(ANY,) * 3,
-        scratch_shapes=[vmem(pair)] + [vmem(blocks)] * 3 + [vmem(blocks, BF16)] * 2
-        + [DMA((slots, 4)), DMA],
-        compiler_params=params(24),
+        scratch_shapes=[vmem(blocks)] * 3 + [vmem(blocks, BF16), DMA((slots, 3)), DMA],
+        compiler_params=params(16),
         cost_estimate=pl.CostEstimate(
             flops=slots * 12 * block_size**3, bytes_accessed=14 * MIB, transcendentals=0
         ),
         name="gram",
-    )(in_hbm(held), in_hbm(second), in_hbm(left_stat), in_hbm(right_stat))
+    )(arrived, in_hbm(second), in_hbm(left_stat), in_hbm(right_stat))
 
     step, new_momentum = pl.pallas_call(
         step_kernel,

time: 94.1 us -> 94.8 us (level)
  waiting for transfers between devices: 1.66 us -> 4.48 us
  Pallas kernels: 17.3 us -> 14.8 us
    all_to_all x1, waiting for transfers between devices: 1.66 us -> 4.48 us  [body(): lax.all_to_all(sums, ('dp', 'tensor'), split_axis=0, concat_axis=0, tiled...]
    pallas_call x2, Pallas kernels: 10.6 us -> 8.17 us  [the longest x1 4.65 us: body(): pl.pallas_call(gram_kernel, out_shape=(hbm(blocks),) * 3, in_specs=[VMEM]...]
  transfers between devices with their start and end apart: 1 -> 1, of which waited for: 1 -> 1; matrix products, arithmetic and copies ran while one was open for 0% -> 0% of each run, Pallas kernels for 8% -> 5%
where the time goes in v2:
time: 94.8 us; the launch traced here: 93.5 us
  blocking collectives  62.7 us (66%)
  Pallas kernels  14.8 us (16%)
  starting transfers between devices  9.19 us (10%)
  waiting for transfers between devices  4.48 us (5%)
  local copies, waits for them, and re-layouts  1.61 us (2%)
    all_to_all x1, blocking collectives, body(): arrived = in_vmem(over_tensor(outgoing))  32.5 us
    all_to_all x1, blocking collectives, body(): returned = over_tensor(step)  30.3 us
    all_to_all x1, starting transfers between devices, body(): lax.all_to_all(sums, ('dp', 'tensor'), split_axis=0, concat_axis=0, tiled...  9.19 us
    pallas_call x1, Pallas kernels, body(): pl.pallas_call(gram_kernel, out_shape=(hbm(blocks),) * 3, in_specs=[VMEM]...  4.65 us
    all_to_all x1, waiting for transfers between devices, body(): lax.all_to_all(sums, ('dp', 'tensor'), split_axis=0, concat_axis=0, tiled...  4.48 us
    pallas_call x1, Pallas kernels, body(): pl.pallas_call(mid_kernel, out_shape=(hbm(pair), hbm((ranks, 2, 128))), i...  3.52 us
    pallas_call x1, Pallas kernels, body(): pl.pallas_call(step_kernel, out_shape=(vmem(pair), hbm(blocks)), in_specs...  2.39 us
    pallas_call x1, Pallas kernels, body(): pl.pallas_call(pack_kernel, out_shape=jax.ShapeDtypeStruct(pair, F32), gr...  2.28 us
  transfers between devices with their start and end apart: 1, of which 1 were waited for; matrix products, arithmetic and copies ran while one was open for 0% of the time, Pallas kernels for 5%

profile of v2, /device:TPU:9, one launch (start us, length us, event | category | flops | bytes accessed | tf_op | source)
XLA Modules:
  0.0 93.5 jit_solution(6012483469712194661)
XLA Ops:
  0.6 2.3 %pack.1 = f32[16,2,32,512]{3,2,1,0:T(8,128)S(1)} custom-call(s32[1,32]{1,0:T(1,128)} %order_ref.3, f32[512,1024]{1,0:T(8,128)} %grad_ref.1), custom_call_target="tpu_custom_call" | custom-call | tf_op jit(solution)/shard_map/pack/pallas_call | solution.py:208
  2.9 0.0 copy-start
  2.9 0.0 copy-start.2
  2.9 0.0 copy-start.3
  3.0 32.5 %all_to_all.15.arrived_ref = f32[16,2,32,512]{3,2,1,0:T(8,128)S(1)} all-to-all(f32[16,2,32,512]{3,2,1,0:T(8,128)S(1)} %pack.1), channel_id=1, replica_groups=mesh['dp'=8,'tensor'=16] {'tensor'}, dimensions={0} | all-to-all | bytes 4194304 | tf_op jit(solution)/shard_map/all_to_all | solution.py:218
  35.4 0.0 copy-done
  35.4 0.0 copy-done.2
  35.4 0.0 copy-done.3
  35.4 3.5 %mid.1 = (f32[16,2,32,512]{3,2,1,0:T(8,128)}, f32[128,2,128]{2,1,0:T(2,128)}) custom-call(f32[16,2,32,512]{3,2,1,0:T(8,128)S(1)} %all_to_all.15.arrived_ref, f32[2,512,512]{2,1,0:T(8,128)S(1)} %copy-done, bf16[2,512,512]{2,1,0:T(8,128)(2,1)S(1)} %copy-done.2, bf16[2,512,512]{2,1,0:T(8,128)(2,1)S(1)} %copy-done.3), custom_call_target="tpu_custom_call" | custom-call | tf_op jit(solution)/shard_map/mid/pallas_call | solution.py:220
  39.0 9.2 %all-to-all-start.1 = ((f32[128,2,128]{2,1,0:T(2,128)}), f32[128,2,128]{2,1,0:T(2,128)S(1)}, u32[]{:S(2)}, u32[]{:S(2)}) async-start(f32[128,2,128]{2,1,0:T(2,128)} %get-tuple-element.14), calls=%async_computation.1 | async-start | bytes 262144 | tf_op jit(solution)/shard_map/all_to_all | solution.py:229
  48.2 4.6 %gram.1 = (f32[2,512,512]{2,1,0:T(8,128)}, f32[2,512,512]{2,1,0:T(8,128)}, f32[2,512,512]{2,1,0:T(8,128)}) custom-call(f32[16,2,32,512]{3,2,1,0:T(8,128)S(1)} %all_to_all.15.arrived_ref, f32[2,512,512]{2,1,0:T(8,128)} %second_ref.3, f32[2,512,512]{2,1,0:T(8,128)} %left_ref.2, f32[2,512,512]{2,1,0:T(8,128)} %right_ref.2), custom_call_target="tpu_custom_call" | custom-call | flops 3221225472 | bytes 14680064 | tf_op jit(solution)/shard_map/gram/pallas_call | solution.py:233
  52.8 4.5 %all-to-all-done.1.sums_ref = f32[128,2,128]{2,1,0:T(2,128)S(1)} async-done(((f32[128,2,128]{2,1,0:T(2,128)}), f32[128,2,128]{2,1,0:T(2,128)S(1)}, u32[]{:S(2)}, u32[]{:S(2)}) %all-to-all-start.1) | async-done | bytes 131104 | tf_op jit(solution)/shard_map/all_to_all | solution.py:229
  57.3 0.0 copy-start.1
  57.3 1.6 %copy-done.1 = f32[16,2,32,512]{3,2,1,0:T(8,128)S(1)} copy-done((f32[16,2,32,512]{3,2,1,0:T(8,128)S(1)}, f32[16,2,32,512]{3,2,1,0:T(8,128)}, u32[]{:S(2)}) %copy-start.1) | copy-done | bytes 2097176
  58.9 2.4 %step.1 = (f32[16,2,32,512]{3,2,1,0:T(8,128)S(1)}, f32[2,512,512]{2,1,0:T(8,128)}) custom-call(f32[128,2,128]{2,1,0:T(2,128)S(1)} %all-to-all-done.1.sums_ref, f32[16,2,32,512]{3,2,1,0:T(8,128)S(1)} %copy-done.1, f32[2,512,512]{2,1,0:T(8,128)} %momentum_ref.1, f32[2,512,512]{2,1,0:T(8,128)} %get-tuple-element.10._), custom_call_target="tpu_custom_call" | custom-call | tf_op jit(solution)/shard_map/step/pallas_call | solution.py:246
  61.3 30.3 %all_to_all.16.moved_ref = f32[16,2,32,512]{3,2,1,0:T(8,128)S(1)} all-to-all(f32[16,2,32,512]{3,2,1,0:T(8,128)S(1)} %get-tuple-element.18), channel_id=1, replica_groups=mesh['dp'=8,'tensor'=16] {'tensor'}, dimensions={0} | all-to-all | bytes 4194304 | tf_op jit(solution)/shard_map/all_to_all | solution.py:255
  91.6 2.0 %unpack.1 = f32[512,1024]{1,0:T(8,128)} custom-call(s32[1,32]{1,0:T(1,128)} %order_ref.3, f32[16,2,32,512]{3,2,1,0:T(8,128)S(1)} %all_to_all.16.moved_ref), custom_call_target="tpu_custom_call" | custom-call | tf_op jit(solution)/shard_map/unpack/pallas_call | solution.py:257
Async XLA Ops:
  2.9 32.5 %copy-start = (f32[2,512,512]{2,1,0:T(8,128)S(1)}, f32[2,512,512]{2,1,0:T(8,128)}, u32[]{:S(2)}) copy-start(f32[2,512,512]{2,1,0:T(8,128)} %second_ref.3) | copy-start | bytes 6291460
  2.9 32.5 %copy-start.2 = (bf16[2,512,512]{2,1,0:T(8,128)(2,1)S(1)}, bf16[2,512,512]{2,1,0:T(8,128)(2,1)}, u32[]{:S(2)}) copy-start(bf16[2,512,512]{2,1,0:T(8,128)(2,1)} %left_ref.3) | copy-start | bytes 3145732
  2.9 32.5 %copy-start.3 = (bf16[2,512,512]{2,1,0:T(8,128)(2,1)S(1)}, bf16[2,512,512]{2,1,0:T(8,128)(2,1)}, u32[]{:S(2)}) copy-start(bf16[2,512,512]{2,1,0:T(8,128)(2,1)} %right_ref.3) | copy-start | bytes 3145732
  39.0 18.3 %all-to-all-start.1 = ((f32[128,2,128]{2,1,0:T(2,128)}), f32[128,2,128]{2,1,0:T(2,128)S(1)}, u32[]{:S(2)}, u32[]{:S(2)}) async-start(f32[128,2,128]{2,1,0:T(2,128)} %get-tuple-element.14), calls=%async_computation.1 | async-start | bytes 262144 | tf_op jit(solution)/shard_map/all_to_all | solution.py:229
  57.3 1.6 %copy-start.1 = (f32[16,2,32,512]{3,2,1,0:T(8,128)S(1)}, f32[16,2,32,512]{3,2,1,0:T(8,128)}, u32[]{:S(2)}) copy-start(f32[16,2,32,512]{3,2,1,0:T(8,128)} %get-tuple-element.15.shampoo_ref) | copy-start | bytes 6291460

commit v3 on v1

--- a/solution.py
+++ b/solution.py
@@ -118,26 +118,40 @@
     return root[0:1, 0:1] / (root[1:2, 0:1] + 1e-06)
 
 
-def gram_kernel(
-    held_ref, second_ref, left_ref, right_ref,
-    new_left_ref, new_right_ref, new_second_ref,
-    held_here, second_here, left_here, right_here, high_ref, low_ref, sems, store_sem,
+def step_kernel(sums_ref, shampoo_ref, momentum_ref, step_ref, here_ref, sem):
+    peers, slots, piece_rows, block_size = shampoo_ref.shape
+    graft = graft_of(sums_ref)
+    count = peers // CHUNKS
+    for peer in range(peers):
+        rows = rows_of(peer, piece_rows)
+        for slot in range(slots):
+            scaled = graft * shampoo_ref[peer, slot]
+            new_momentum = 0.9 * momentum_ref[slot, rows, :] + scaled
+            here_ref[peer, slot] = -(0.9 * new_momentum + scaled)
+        if peer % count == count - 1:
+            part = pl.ds(peer - count + 1, count)
+            started(here_ref.at[part], step_ref.at[part], sem)
+    wait_all(here_ref, sem)
+
+
+def rest_kernel(
+    held_ref, second_ref, left_ref, right_ref, momentum_ref, step_ref,
+    new_left_ref, new_right_ref, new_second_ref, new_momentum_ref,
+    held_here, second_here, left_here, right_here, momentum_here, step_here, high_ref, low_ref,
+    sems, store_sem,
 ):
     peers, slots, piece_rows, block_size = held_ref.shape
-    loads = [
-        [
-            started(source.at[(*at, slot)], target.at[(*at, slot)], sems.at[slot, k])
-            for k, (source, target, at) in enumerate(
-                (
-                    (held_ref, held_here, (slice(None),)),
-                    (left_ref, left_here, ()),
-                    (right_ref, right_here, ()),
-                    (second_ref, second_here, ()),
-                )
-            )
-        ]
-        for slot in range(slots)
-    ]
+    loads = []
+    for slot in range(slots):
+        pairs = (
+            (left_ref.at[slot], left_here.at[slot]),
+            (right_ref.at[slot], right_here.at[slot]),
+            (second_ref.at[slot], second_here.at[slot]),
+            (momentum_ref.at[slot], momentum_here.at[slot]),
+            (step_ref.at[:, slot], step_here.at[:, slot]),
+            (held_ref.at[:, slot], held_here.at[:, slot]),
+        )[::-1]
+        loads.append([started(*pair, sems.at[slot, k]) for k, pair in enumerate(pairs)])
     scale = 0.1 / block_size
     half = block_size // 2
     for slot in range(slots):
@@ -156,7 +170,7 @@
                 dimension_numbers=(((1 - k,), (1 - k,)), ((), ())),
                 preferred_element_type=F32,
             )
-            loads[slot][1 + k].wait()
+            loads[slot][5 - k].wait()
             for part in range(2):
                 cut = slice(part * half, (part + 1) * half)
                 at = (slot, cut, slice(None)) if k == 0 else (slot, slice(None), cut)
@@ -167,41 +181,19 @@
                 )
                 here[slot, cut, :] = 0.9 * here[slot, cut, :] + scale * gram
             started(here.at[slot], ref.at[slot], store_sem)
-        loads[slot][3].wait()
+        for load in loads[slot][1:4]:
+            load.wait()
         for peer in range(peers):
             rows = rows_of(peer, piece_rows)
             held = held_here[peer, slot]
             second_here[slot, rows, :] = 0.99 * second_here[slot, rows, :] + 0.01 * held * held
+            momentum_here[slot, rows, :] = (
+                0.9 * momentum_here[slot, rows, :] - step_here[peer, slot]
+            ) * (1.0 / 1.9)
         started(second_here.at[slot], new_second_ref.at[slot], store_sem)
-    for here in (left_here, right_here, second_here):
+        started(momentum_here.at[slot], new_momentum_ref.at[slot], store_sem)
+    for here in (left_here, right_here, second_here, momentum_here):
         wait_all(here, store_sem)
-
-
-def step_kernel(
-    sums_ref, shampoo_ref, momentum_ref, _, step_ref, new_momentum_ref, here_ref, sems, store_sem
-):
-    peers, slots, piece_rows, block_size = shampoo_ref.shape
-    count = peers // CHUNKS
-    parts = [
-        (slot, chunk, (slot, pl.ds(chunk * count * piece_rows, count * piece_rows)))
-        for chunk in range(CHUNKS)
-        for slot in range(slots)
-    ]
-    loads = [
-        started(momentum_ref.at[at], here_ref.at[at], sems.at[slot, chunk])
-        for slot, chunk, at in parts
-    ]
-    graft = graft_of(sums_ref)
-    for load, (slot, chunk, at) in zip(loads, parts):
-        load.wait()
-        for peer in range(chunk * count, (chunk + 1) * count):
-            rows = rows_of(peer, piece_rows)
-            scaled = graft * shampoo_ref[peer, slot]
-            new_momentum = 0.9 * here_ref[slot, rows, :] + scaled
-            here_ref[slot, rows, :] = new_momentum
-            step_ref[peer, slot] = -(0.9 * new_momentum + scaled)
-        started(here_ref.at[at], new_momentum_ref.at[at], store_sem)
-    wait_all(here_ref, store_sem)
 
 
 def body(grad, owner_order, left_stat, right_stat, left_root, right_root, momentum, second):
@@ -232,7 +224,7 @@
 
     shampoo, held, sums = pl.pallas_call(
         mid_kernel,
-        out_shape=(vmem(pair), hbm(pair), hbm((ranks, 2, 128))),
+        out_shape=(vmem(pair), hbm(pair), jax.ShapeDtypeStruct((ranks, 2, 128), F32)),
         in_specs=[VMEM] * 4,
         out_specs=(VMEM, ANY, VMEM),
         scratch_shapes=[vmem(blocks, BF16), DMA],
@@ -243,39 +235,41 @@
         sums, ("dp", "tensor"), split_axis=0, concat_axis=0, tiled=True
     )
 
-    new_left, new_right, new_second = pl.pallas_call(
-        gram_kernel,
-        out_shape=(hbm(blocks),) * 3,
-        in_specs=[ANY] * 4,
-        out_specs=(ANY,) * 3,
-        scratch_shapes=[vmem(pair)] + [vmem(blocks)] * 3 + [vmem(blocks, BF16)] * 2
-        + [DMA((slots, 4)), DMA],
+    step = pl.pallas_call(
+        step_kernel,
+        out_shape=hbm(pair),
+        in_specs=[VMEM] * 3,
+        out_specs=ANY,
+        scratch_shapes=[vmem(pair), DMA],
+        compiler_params=params(8),
+        name="step",
+    )(sums, in_vmem(shampoo), in_vmem(momentum))
+    returned = over_tensor(step)
+
+    new_left, new_right, new_second, new_momentum = pl.pallas_call(
+        rest_kernel,
+        out_shape=(hbm(blocks),) * 4,
+        in_specs=[ANY] * 6,
+        out_specs=(ANY,) * 4,
+        scratch_shapes=[vmem(pair)] + [vmem(blocks)] * 4 + [vmem(pair)]
+        + [vmem(blocks, BF16)] * 2 + [DMA((slots, 6)), DMA],
         compiler_params=params(24),
         cost_estimate=pl.CostEstimate(
-            flops=slots * 12 * block_size**3, bytes_accessed=14 * MIB, transcendentals=0
+            flops=slots * 12 * block_size**3, bytes_accessed=18 * MIB, transcendentals=0
         ),
-        name="gram",
-    )(in_hbm(held), in_hbm(second), in_hbm(left_stat), in_hbm(right_stat))
-
-    step, new_momentum = pl.pallas_call(
-        step_kernel,
-        out_shape=(vmem(pair), hbm(blocks)),
-        in_specs=[VMEM, VMEM, ANY, ANY],
-        out_specs=(VMEM, ANY),
-        scratch_shapes=[vmem(blocks), DMA((slots, CHUNKS)), DMA],
-        compiler_params=params(8),
-        name="step",
-    )(sums, in_vmem(shampoo), in_hbm(momentum), in_hbm(new_second))
-    returned = over_tensor(step)
+        name="rest",
+    )(
+        in_hbm(held), in_hbm(second), in_hbm(left_stat), in_hbm(right_stat),
+        in_hbm(momentum), in_hbm(step),
+    )
 
     update = pl.pallas_call(
         unpack_kernel,
         out_shape=hbm(grad.shape),
-        grid_spec=pltpu.PrefetchScalarGridSpec(
-            num_scalar_prefetch=1, grid=(1,), in_specs=[ANY], out_specs=ANY,
-            scratch_shapes=[DMA],
-        ),
-        compiler_params=params(2),
+        in_specs=[pl.BlockSpec(memory_space=pltpu.SMEM), VMEM],
+        out_specs=ANY,
+        scratch_shapes=[DMA],
+        compiler_params=params(8),
         name="unpack",
     )(order, in_vmem(returned))
     return (new_left, new_right, new_momentum, new_second, update)

time: 94.1 us -> 93.8 us (level)
  waiting for transfers between devices: 1.66 us -> 19.6 us
  blocking collectives: 62.7 us -> 50.8 us
  starting transfers between devices: 9.19 us -> 4.95 us
  local copies, waits for them, and re-layouts: 1.34 us -> 0.03 us
    all_to_all x1, waiting for transfers between devices: 1.66 us -> 19.6 us  [body(): returned = over_tensor(step)]
    all_to_all x1, blocking collectives: 30.3 us -> 18.3 us  [body(): lax.all_to_all(sums, ('dp', 'tensor'), split_axis=0, concat_axis=0, tiled...]
    all_to_all x1, starting transfers between devices: 9.19 us -> 4.95 us  [body(): returned = over_tensor(step)]
    unnamed x10 -> x8, local copies, waits for them, and re-layouts: 1.34 us -> 0.03 us
  transfers between devices with their start and end apart: 1 -> 1, of which waited for: 1 -> 1; matrix products, arithmetic and copies ran while one was open for 0% -> 0% of each run, Pallas kernels for 8% -> 10%
where the time goes in v3:
time: 93.8 us; the launch traced here: 93.5 us
  blocking collectives  50.8 us (54%)
  waiting for transfers between devices  19.6 us (21%)
  Pallas kernels  17.5 us (19%)
  starting transfers between devices  4.95 us (5%)
    all_to_all x1, blocking collectives, body(): arrived = over_tensor(outgoing)  32.5 us
    all_to_all x1, waiting for transfers between devices, body(): returned = over_tensor(step)  19.6 us
    all_to_all x1, blocking collectives, body(): lax.all_to_all(sums, ('dp', 'tensor'), split_axis=0, concat_axis=0, tiled...  18.3 us
    pallas_call x1, Pallas kernels, body(): pl.pallas_call(rest_kernel, out_shape=(hbm(blocks),) * 4, in_specs=[ANY]...  9.1 us
    all_to_all x1, starting transfers between devices, body(): returned = over_tensor(step)  4.95 us
    pallas_call x1, Pallas kernels, body(): pl.pallas_call(mid_kernel, out_shape=(vmem(pair), hbm(pair), jax.ShapeDty...  2.52 us
    pallas_call x1, Pallas kernels, body(): pl.pallas_call(pack_kernel, out_shape=jax.ShapeDtypeStruct(pair, F32), gr...  2.28 us
    pallas_call x1, Pallas kernels, body(): pl.pallas_call(unpack_kernel, out_shape=hbm(grad.shape), in_specs=[pl.Blo...  1.96 us
  transfers between devices with their start and end apart: 1, of which 1 were waited for; matrix products, arithmetic and copies ran while one was open for 0% of the time, Pallas kernels for 10%

profile of v3, /device:TPU:9, one launch (start us, length us, event | category | flops | bytes accessed | tf_op | source)
XLA Modules:
  0.0 93.5 jit_solution(16642280873029986116)
XLA Ops:
  0.6 2.3 %pack.1 = f32[16,2,32,512]{3,2,1,0:T(8,128)S(1)} custom-call(s32[1,32]{1,0:T(1,128)} %order_ref.3, f32[512,1024]{1,0:T(8,128)} %grad_ref.1), custom_call_target="tpu_custom_call" | custom-call | tf_op jit(solution)/shard_map/pack/pallas_call | solution.py:213
  2.9 0.0 copy-start
  2.9 0.0 copy-start.2
  2.9 0.0 copy-start.3
  3.0 32.5 %all_to_all.15.arrived_ref = f32[16,2,32,512]{3,2,1,0:T(8,128)S(1)} all-to-all(f32[16,2,32,512]{3,2,1,0:T(8,128)S(1)} %pack.1), channel_id=1, replica_groups=mesh['dp'=8,'tensor'=16] {'tensor'}, dimensions={0} | all-to-all | bytes 4194304 | tf_op jit(solution)/shard_map/all_to_all | solution.py:223
  35.4 0.0 copy-done
  35.4 0.0 copy-done.2
  35.4 0.0 copy-done.3
  35.4 0.0 copy-start.1
  35.4 2.5 %mid.1 = (f32[16,2,32,512]{3,2,1,0:T(8,128)S(1)}, f32[16,2,32,512]{3,2,1,0:T(8,128)}, f32[128,2,128]{2,1,0:T(2,128)S(1)}) custom-call(f32[16,2,32,512]{3,2,1,0:T(8,128)S(1)} %all_to_all.15.arrived_ref, f32[2,512,512]{2,1,0:T(8,128)S(1)} %copy-done, bf16[2,512,512]{2,1,0:T(8,128)(2,1)S(1)} %copy-done.2, bf16[2,512,512]{2,1,0:T(8,128)(2,1)S(1)} %copy-done.3), custom_call_target="tpu_custom_call" | custom-call | tf_op jit(solution)/shard_map/mid/pallas_call | solution.py:225
  38.0 18.3 %all_to_all.16.sums_ref = f32[128,2,128]{2,1,0:T(2,128)S(1)} all-to-all(f32[128,2,128]{2,1,0:T(2,128)S(1)} %get-tuple-element.13), channel_id=1, replica_groups=mesh['dp'=8,'tensor'=16] {'dp','tensor'}, dimensions={0} | all-to-all | bytes 262144 | tf_op jit(solution)/shard_map/all_to_all | solution.py:234
  56.3 0.0 copy-done.1
  56.3 1.6 %step.1.step_ref = f32[16,2,32,512]{3,2,1,0:T(8,128)} custom-call(f32[128,2,128]{2,1,0:T(2,128)S(1)} %all_to_all.16.sums_ref, f32[16,2,32,512]{3,2,1,0:T(8,128)S(1)} %get-tuple-element.14.shampoo_ref, f32[2,512,512]{2,1,0:T(8,128)S(1)} %copy-done.1), custom_call_target="tpu_custom_call" | custom-call | tf_op jit(solution)/shard_map/step/pallas_call | solution.py:238
  57.9 5.0 %all-to-all-start.2 = ((f32[16,2,32,512]{3,2,1,0:T(8,128)}), f32[16,2,32,512]{3,2,1,0:T(8,128)S(1)}, u32[]{:S(2)}, u32[]{:S(2)}) async-start(f32[16,2,32,512]{3,2,1,0:T(8,128)} %step.1.step_ref), calls=%async_computation.2 | async-start | bytes 4194304 | tf_op jit(solution)/shard_map/all_to_all | solution.py:247
  62.9 9.1 %rest.1 = (f32[2,512,512]{2,1,0:T(8,128)}, f32[2,512,512]{2,1,0:T(8,128)}, f32[2,512,512]{2,1,0:T(8,128)}, f32[2,512,512]{2,1,0:T(8,128)}) custom-call(f32[16,2,32,512]{3,2,1,0:T(8,128)} %get-tuple-element.12.held_ref, f32[2,512,512]{2,1,0:T(8,128)} %second_ref.3, f32[2,512,512]{2,1,0:T(8,128)} %left_ref.3, f32[2,512,512]{2,1,0:T(8,128)} %right_ref.3, ...), custom_call_target="tpu_custom_call" | custom-call | flops 3221225472 | bytes 18874368 | tf_op jit(solution)/shard_map/rest/pallas_call | solution.py:249
  72.0 19.6 %all-to-all-done.2.moved_ref = f32[16,2,32,512]{3,2,1,0:T(8,128)S(1)} async-done(((f32[16,2,32,512]{3,2,1,0:T(8,128)}), f32[16,2,32,512]{3,2,1,0:T(8,128)S(1)}, u32[]{:S(2)}, u32[]{:S(2)}) %all-to-all-start.2) | async-done | bytes 2097184 | tf_op jit(solution)/shard_map/all_to_all | solution.py:247
  91.6 2.0 %unpack.1 = f32[512,1024]{1,0:T(8,128)} custom-call(s32[1,32]{1,0:T(1,128)} %order_ref.3, f32[16,2,32,512]{3,2,1,0:T(8,128)S(1)} %all-to-all-done.2.moved_ref), custom_call_target="tpu_custom_call" | custom-call | tf_op jit(solution)/shard_map/unpack/pallas_call | solution.py:266
Async XLA Ops:
  2.9 32.5 %copy-start = (f32[2,512,512]{2,1,0:T(8,128)S(1)}, f32[2,512,512]{2,1,0:T(8,128)}, u32[]{:S(2)}) copy-start(f32[2,512,512]{2,1,0:T(8,128)} %second_ref.3) | copy-start | bytes 6291460
  2.9 32.5 %copy-start.2 = (bf16[2,512,512]{2,1,0:T(8,128)(2,1)S(1)}, bf16[2,512,512]{2,1,0:T(8,128)(2,1)}, u32[]{:S(2)}) copy-start(bf16[2,512,512]{2,1,0:T(8,128)(2,1)} %left_ref.2) | copy-start | bytes 3145732
  2.9 32.5 %copy-start.3 = (bf16[2,512,512]{2,1,0:T(8,128)(2,1)S(1)}, bf16[2,512,512]{2,1,0:T(8,128)(2,1)}, u32[]{:S(2)}) copy-start(bf16[2,512,512]{2,1,0:T(8,128)(2,1)} %right_ref.2) | copy-start | bytes 3145732
  35.4 20.9 %copy-start.1 = (f32[2,512,512]{2,1,0:T(8,128)S(1)}, f32[2,512,512]{2,1,0:T(8,128)}, u32[]{:S(2)}) copy-start(f32[2,512,512]{2,1,0:T(8,128)} %momentum_ref.3) | copy-start | bytes 6291460
  57.9 33.6 %all-to-all-start.2 = ((f32[16,2,32,512]{3,2,1,0:T(8,128)}), f32[16,2,32,512]{3,2,1,0:T(8,128)S(1)}, u32[]{:S(2)}, u32[]{:S(2)}) async-start(f32[16,2,32,512]{3,2,1,0:T(8,128)} %step.1.step_ref), calls=%async_computation.2 | async-start | bytes 4194304 | tf_op jit(solution)/shard_map/all_to_all | solution.py:247

commit v4 on v3

--- a/solution.py
+++ b/solution.py
@@ -2,6 +2,7 @@
 
 import jax
 import jax.numpy as jnp
+import numpy as np
 from jax import lax
 from jax.experimental import pallas as pl
 from jax.experimental.pallas import tpu as pltpu
@@ -16,6 +17,23 @@
 CHUNKS = 4
 
 
+FINE = (("z", 4), ("yh", 2), ("x", 4), ("yl", 2), ("core", 2))
+DP, TENSOR = ("z", "yh"), ("x", "yl", "core")
+OUT_ORDER, BACK_ORDER = TENSOR, TENSOR
+
+
+def places_of(order):
+    sizes = dict(FINE)
+    places = []
+    for at in np.ndindex(*(sizes[axis] for axis in order)):
+        where = dict(zip(order, at))
+        place = 0
+        for axis in TENSOR:
+            place = place * sizes[axis] + where[axis]
+        places.append(place)
+    return places
+
+
 def in_vmem(x):
     return pltpu.with_memory_space_constraint(x, pltpu.VMEM)
 
@@ -53,22 +71,36 @@
     return slice(peer * piece_rows, (peer + 1) * piece_rows)
 
 
-def pack_kernel(order_ref, grad_ref, out_ref, sem):
+def pack_kernel(
+    places, order_ref, grad_ref, out_ref, here_ref, order_here, index_ref, sems, order_sem
+):
     peers, slots, piece_rows, block_size = out_ref.shape
+    table = started(order_ref, order_here, order_sem)
+    col_blocks = grad_ref.shape[1] // block_size
+    chunk_rows = grad_ref.shape[0] // sems.shape[0]
+    loads = []
+    for chunk in range(sems.shape[0]):
+        rows = pl.ds(chunk * chunk_rows, chunk_rows)
+        loads.append(started(grad_ref.at[rows], here_ref.at[rows], sems.at[chunk]))
+    table.wait()
     for peer in range(peers):
         for slot in range(slots):
-            block = order_ref[0, peer * slots + slot]
-            started(
-                piece_of(grad_ref, block, piece_rows, block_size), out_ref.at[peer, slot], sem
-            )
-    wait_all(out_ref, sem)
-
-
-def unpack_kernel(order_ref, moved_ref, out_ref, sem):
+            index_ref[order_here[0, places[peer] * slots + slot]] = peer * slots + slot
+    for chunk, load in enumerate(loads):
+        load.wait()
+        for row in range(chunk * chunk_rows, (chunk + 1) * chunk_rows, piece_rows):
+            for column in range(col_blocks):
+                at = index_ref[row // piece_rows * col_blocks + column]
+                out_ref[at // slots, at % slots] = here_ref[
+                    row : row + piece_rows, column * block_size : (column + 1) * block_size
+                ]
+
+
+def unpack_kernel(places, order_ref, moved_ref, out_ref, sem):
     peers, slots, piece_rows, block_size = moved_ref.shape
     for peer in range(peers):
         for slot in range(slots):
-            block = order_ref[0, peer * slots + slot]
+            block = order_ref[0, places[peer] * slots + slot]
             started(
                 moved_ref.at[peer, slot], piece_of(out_ref, block, piece_rows, block_size), sem
             )
@@ -80,7 +112,7 @@
 
 
 def mid_kernel(
-    arrived_ref, second_ref, left_ref, right_ref, shampoo_ref, held_ref, sums_ref, low_ref, sem
+    places, arrived_ref, second_ref, left_ref, right_ref, shampoo_ref, held_ref, sums_ref, low_ref, sem
 ):
     peers, slots, piece_rows, block_size = arrived_ref.shape
     half = block_size // 2
@@ -90,7 +122,7 @@
     shampoo_sq = jnp.zeros((8, block_size), F32)
     for slot in range(slots):
         for peer in range(peers):
-            rows = rows_of(peer, piece_rows)
+            rows = rows_of(places[peer], piece_rows)
             held = arrived_ref[peer, slot]
             low_ref[slot, rows, :] = held.astype(BF16)
             new_second = 0.99 * second_ref[slot, rows, :] + 0.01 * held * held
@@ -118,14 +150,14 @@
     return root[0:1, 0:1] / (root[1:2, 0:1] + 1e-06)
 
 
-def step_kernel(sums_ref, shampoo_ref, momentum_ref, step_ref, here_ref, sem):
+def step_kernel(places, sums_ref, shampoo_ref, momentum_ref, step_ref, here_ref, sem):
     peers, slots, piece_rows, block_size = shampoo_ref.shape
     graft = graft_of(sums_ref)
-    count = peers // CHUNKS
+    count = peers // (2 * CHUNKS)
     for peer in range(peers):
-        rows = rows_of(peer, piece_rows)
+        rows = rows_of(places[peer], piece_rows)
         for slot in range(slots):
-            scaled = graft * shampoo_ref[peer, slot]
+            scaled = graft * shampoo_ref[places[peer], slot]
             new_momentum = 0.9 * momentum_ref[slot, rows, :] + scaled
             here_ref[peer, slot] = -(0.9 * new_momentum + scaled)
         if peer % count == count - 1:
@@ -135,7 +167,7 @@
 
 
 def rest_kernel(
-    held_ref, second_ref, left_ref, right_ref, momentum_ref, step_ref,
+    out_places, back_places, held_ref, second_ref, left_ref, right_ref, momentum_ref, step_ref,
     new_left_ref, new_right_ref, new_second_ref, new_momentum_ref,
     held_here, second_here, left_here, right_here, momentum_here, step_here, high_ref, low_ref,
     sems, store_sem,
@@ -157,7 +189,7 @@
     for slot in range(slots):
         loads[slot][0].wait()
         for peer in range(peers):
-            rows = rows_of(peer, piece_rows)
+            rows = rows_of(out_places[peer], piece_rows)
             held = held_here[peer, slot]
             high = held.astype(BF16)
             high_ref[slot, rows, :] = high
@@ -184,9 +216,10 @@
         for load in loads[slot][1:4]:
             load.wait()
         for peer in range(peers):
-            rows = rows_of(peer, piece_rows)
+            rows = rows_of(out_places[peer], piece_rows)
             held = held_here[peer, slot]
             second_here[slot, rows, :] = 0.99 * second_here[slot, rows, :] + 0.01 * held * held
+            rows = rows_of(back_places[peer], piece_rows)
             momentum_here[slot, rows, :] = (
                 0.9 * momentum_here[slot, rows, :] - step_here[peer, slot]
             ) * (1.0 / 1.9)
@@ -198,32 +231,32 @@
 
 def body(grad, owner_order, left_stat, right_stat, left_root, right_root, momentum, second):
     slots, block_size = left_stat.shape[0], left_stat.shape[1]
-    peers = lax.axis_size("tensor")
-    ranks = peers * lax.axis_size("dp")
+    peers, ranks = lax.axis_size(TENSOR), lax.axis_size(DP + TENSOR)
+    out_places, back_places = places_of(OUT_ORDER), places_of(BACK_ORDER)
     piece_rows = block_size // peers
     pair = (peers, slots, piece_rows, block_size)
     blocks = (slots, block_size, block_size)
     hbm = lambda shape: pltpu.HBM(shape, F32)
     vmem = lambda shape, dtype=F32: pltpu.VMEM(shape, dtype)
-    over_tensor = functools.partial(
-        lax.all_to_all, axis_name="tensor", split_axis=0, concat_axis=0, tiled=True
-    )
+    exchange = functools.partial(lax.all_to_all, split_axis=0, concat_axis=0, tiled=True)
     order = in_hbm(owner_order)
 
     outgoing = pl.pallas_call(
-        pack_kernel,
-        out_shape=jax.ShapeDtypeStruct(pair, F32),
-        grid_spec=pltpu.PrefetchScalarGridSpec(
-            num_scalar_prefetch=1, grid=(1,), in_specs=[ANY], out_specs=ANY,
-            scratch_shapes=[DMA],
-        ),
-        compiler_params=params(2),
+        functools.partial(pack_kernel, out_places),
+        out_shape=vmem(pair),
+        in_specs=[ANY, ANY],
+        out_specs=VMEM,
+        scratch_shapes=[
+            vmem(grad.shape), pltpu.SMEM(owner_order.shape, jnp.int32),
+            pltpu.SMEM((peers * slots,), jnp.int32), DMA((2 * CHUNKS,)), DMA,
+        ],
+        compiler_params=params(8),
         name="pack",
     )(order, in_hbm(grad))
-    arrived = over_tensor(outgoing)
+    arrived = exchange(outgoing, OUT_ORDER)
 
     shampoo, held, sums = pl.pallas_call(
-        mid_kernel,
+        functools.partial(mid_kernel, out_places),
         out_shape=(vmem(pair), hbm(pair), jax.ShapeDtypeStruct((ranks, 2, 128), F32)),
         in_specs=[VMEM] * 4,
         out_specs=(VMEM, ANY, VMEM),
@@ -231,12 +264,10 @@
         compiler_params=params(16),
         name="mid",
     )(in_vmem(arrived), in_vmem(second), in_vmem(left_root), in_vmem(right_root))
-    sums = lax.all_to_all(
-        sums, ("dp", "tensor"), split_axis=0, concat_axis=0, tiled=True
-    )
+    sums = exchange(sums, DP + TENSOR)
 
     step = pl.pallas_call(
-        step_kernel,
+        functools.partial(step_kernel, back_places),
         out_shape=hbm(pair),
         in_specs=[VMEM] * 3,
         out_specs=ANY,
@@ -244,10 +275,10 @@
         compiler_params=params(8),
         name="step",
     )(sums, in_vmem(shampoo), in_vmem(momentum))
-    returned = over_tensor(step)
+    returned = exchange(step, BACK_ORDER)
 
     new_left, new_right, new_second, new_momentum = pl.pallas_call(
-        rest_kernel,
+        functools.partial(rest_kernel, out_places, back_places),
         out_shape=(hbm(blocks),) * 4,
         in_specs=[ANY] * 6,
         out_specs=(ANY,) * 4,
@@ -264,7 +295,7 @@
     )
 
     update = pl.pallas_call(
-        unpack_kernel,
+        functools.partial(unpack_kernel, back_places),
         out_shape=hbm(grad.shape),
         in_specs=[pl.BlockSpec(memory_space=pltpu.SMEM), VMEM],
         out_specs=ANY,
@@ -276,11 +307,13 @@
 
 
 def solution(mesh):
-    owned = P(("dp", "tensor"), None, None)
+    names, sizes = zip(*FINE)
+    fine = jax.sharding.Mesh(mesh.devices.reshape(sizes), names)
+    owned = P(DP + TENSOR, None, None)
     return jax.shard_map(
         body,
-        mesh=mesh,
-        in_specs=(P("tensor", "dp"), P("dp", None)) + (owned,) * 6,
-        out_specs=(owned,) * 4 + (P("tensor", "dp"),),
+        mesh=fine,
+        in_specs=(P(TENSOR, DP), P(DP, None)) + (owned,) * 6,
+        out_specs=(owned,) * 4 + (P(TENSOR, DP),),
         check_vma=False,
     )

time: 93.8 us -> 93 us (level)
  no operation moved by 1% of the time
where the time goes in v4:
time: 93 us; the launch traced here: 92.8 us
  blocking collectives  50.8 us (55%)
  waiting for transfers between devices  19.6 us (21%)
  Pallas kernels  16.8 us (18%)
  starting transfers between devices  4.95 us (5%)
    all_to_all x1, blocking collectives, body(): arrived = exchange(outgoing, OUT_ORDER)  32.5 us
    all_to_all x1, waiting for transfers between devices, body(): returned = exchange(step, BACK_ORDER)  19.6 us
    all_to_all x1, blocking collectives, body(): sums = exchange(sums, DP + TENSOR)  18.3 us
    pallas_call x1, Pallas kernels, body(): pl.pallas_call(functools.partial(rest_kernel, out_places, back_places), o...  9.1 us
    all_to_all x1, starting transfers between devices, body(): returned = exchange(step, BACK_ORDER)  4.95 us
    pallas_call x1, Pallas kernels, body(): pl.pallas_call(functools.partial(mid_kernel, out_places), out_shape=(vmem...  2.53 us
    pallas_call x1, Pallas kernels, body(): pl.pallas_call(functools.partial(unpack_kernel, back_places), out_shape=h...  1.96 us
  transfers between devices with their start and end apart: 1, of which 1 were waited for; matrix products, arithmetic and copies ran while one was open for 0% of the time, Pallas kernels for 10%

profile of v4, /device:TPU:9, one launch (start us, length us, event | category | flops | bytes accessed | tf_op | source)
XLA Modules:
  0.0 92.8 jit_solution(10272468643455428179)
XLA Ops:
  0.6 1.6 %pack.1 = f32[16,2,32,512]{3,2,1,0:T(8,128)S(1)} custom-call(s32[1,32]{1,0:T(1,128)} %order_ref.3, f32[512,1024]{1,0:T(8,128)} %grad_ref.1), custom_call_target="tpu_custom_call" | custom-call | tf_op jit(solution)/shard_map/pack/pallas_call | solution.py:244
  2.3 0.0 copy-start
  2.3 0.0 copy-start.2
  2.3 0.0 copy-start.3
  2.3 32.5 %all_to_all.15.arrived_ref = f32[16,2,32,512]{3,2,1,0:T(8,128)S(1)} all-to-all(f32[16,2,32,512]{3,2,1,0:T(8,128)S(1)} %pack.1), channel_id=1, replica_groups=mesh['z'=4,'yh'=2,'x'=4,'yl'=2,'core'=2] {'x','yl','core'}, dimensions={0} | all-to-all | bytes 4194304 | tf_op jit(solution)/shard_map/all_to_all | solution.py:256
  34.7 0.0 copy-done
  34.7 0.0 copy-done.2
  34.7 0.0 copy-done.3
  34.8 0.0 copy-start.1
  34.8 2.5 %mid.1 = (f32[16,2,32,512]{3,2,1,0:T(8,128)S(1)}, f32[16,2,32,512]{3,2,1,0:T(8,128)}, f32[128,2,128]{2,1,0:T(2,128)S(1)}) custom-call(f32[16,2,32,512]{3,2,1,0:T(8,128)S(1)} %all_to_all.15.arrived_ref, f32[2,512,512]{2,1,0:T(8,128)S(1)} %copy-done, bf16[2,512,512]{2,1,0:T(8,128)(2,1)S(1)} %copy-done.2, bf16[2,512,512]{2,1,0:T(8,128)(2,1)S(1)} %copy-done.3), custom_call_target="tpu_custom_call" | custom-call | tf_op jit(solution)/shard_map/mid/pallas_call | solution.py:258
  37.3 18.3 %all_to_all.16.sums_ref = f32[128,2,128]{2,1,0:T(2,128)S(1)} all-to-all(f32[128,2,128]{2,1,0:T(2,128)S(1)} %get-tuple-element.13), channel_id=1, replica_groups=mesh['z'=4,'yh'=2,'x'=4,'yl'=2,'core'=2] {'z','yh','x','yl','core'}, dimensions={0} | all-to-all | bytes 262144 | tf_op jit(solution)/shard_map/all_to_all | solution.py:267
  55.6 0.0 copy-done.1
  55.6 1.6 %step.1.step_ref = f32[16,2,32,512]{3,2,1,0:T(8,128)} custom-call(f32[128,2,128]{2,1,0:T(2,128)S(1)} %all_to_all.16.sums_ref, f32[16,2,32,512]{3,2,1,0:T(8,128)S(1)} %get-tuple-element.14.shampoo_ref, f32[2,512,512]{2,1,0:T(8,128)S(1)} %copy-done.1), custom_call_target="tpu_custom_call" | custom-call | tf_op jit(solution)/shard_map/step/pallas_call | solution.py:269
  57.2 5.0 %all-to-all-start.2 = ((f32[16,2,32,512]{3,2,1,0:T(8,128)}), f32[16,2,32,512]{3,2,1,0:T(8,128)S(1)}, u32[]{:S(2)}, u32[]{:S(2)}) async-start(f32[16,2,32,512]{3,2,1,0:T(8,128)} %step.1.step_ref), calls=%async_computation.2 | async-start | bytes 4194304 | tf_op jit(solution)/shard_map/all_to_all | solution.py:278
  62.2 9.1 %rest.1 = (f32[2,512,512]{2,1,0:T(8,128)}, f32[2,512,512]{2,1,0:T(8,128)}, f32[2,512,512]{2,1,0:T(8,128)}, f32[2,512,512]{2,1,0:T(8,128)}) custom-call(f32[16,2,32,512]{3,2,1,0:T(8,128)} %get-tuple-element.12.held_ref, f32[2,512,512]{2,1,0:T(8,128)} %second_ref.3, f32[2,512,512]{2,1,0:T(8,128)} %left_ref.3, f32[2,512,512]{2,1,0:T(8,128)} %right_ref.3, ...), custom_call_target="tpu_custom_call" | custom-call | flops 3221225472 | bytes 18874368 | tf_op jit(solution)/shard_map/rest/pallas_call | solution.py:280
  71.3 19.6 %all-to-all-done.2.moved_ref = f32[16,2,32,512]{3,2,1,0:T(8,128)S(1)} async-done(((f32[16,2,32,512]{3,2,1,0:T(8,128)}), f32[16,2,32,512]{3,2,1,0:T(8,128)S(1)}, u32[]{:S(2)}, u32[]{:S(2)}) %all-to-all-start.2) | async-done | bytes 2097184 | tf_op jit(solution)/shard_map/all_to_all | solution.py:278
  90.8 2.0 %unpack.1 = f32[512,1024]{1,0:T(8,128)} custom-call(s32[1,32]{1,0:T(1,128)} %order_ref.3, f32[16,2,32,512]{3,2,1,0:T(8,128)S(1)} %all-to-all-done.2.moved_ref), custom_call_target="tpu_custom_call" | custom-call | tf_op jit(solution)/shard_map/unpack/pallas_call | solution.py:297
Async XLA Ops:
  2.3 32.5 %copy-start = (f32[2,512,512]{2,1,0:T(8,128)S(1)}, f32[2,512,512]{2,1,0:T(8,128)}, u32[]{:S(2)}) copy-start(f32[2,512,512]{2,1,0:T(8,128)} %second_ref.3) | copy-start | bytes 6291460
  2.3 32.5 %copy-start.2 = (bf16[2,512,512]{2,1,0:T(8,128)(2,1)S(1)}, bf16[2,512,512]{2,1,0:T(8,128)(2,1)}, u32[]{:S(2)}) copy-start(bf16[2,512,512]{2,1,0:T(8,128)(2,1)} %left_ref.2) | copy-start | bytes 3145732
  2.3 32.5 %copy-start.3 = (bf16[2,512,512]{2,1,0:T(8,128)(2,1)S(1)}, bf16[2,512,512]{2,1,0:T(8,128)(2,1)}, u32[]{:S(2)}) copy-start(bf16[2,512,512]{2,1,0:T(8,128)(2,1)} %right_ref.2) | copy-start | bytes 3145732
  34.8 20.9 %copy-start.1 = (f32[2,512,512]{2,1,0:T(8,128)S(1)}, f32[2,512,512]{2,1,0:T(8,128)}, u32[]{:S(2)}) copy-start(f32[2,512,512]{2,1,0:T(8,128)} %momentum_ref.3) | copy-start | bytes 6291460
  57.2 33.6 %all-to-all-start.2 = ((f32[16,2,32,512]{3,2,1,0:T(8,128)}), f32[16,2,32,512]{3,2,1,0:T(8,128)S(1)}, u32[]{:S(2)}, u32[]{:S(2)}) async-start(f32[16,2,32,512]{3,2,1,0:T(8,128)} %step.1.step_ref), calls=%async_computation.2 | async-start | bytes 4194304 | tf_op jit(solution)/shard_map/all_to_all | solution.py:278

commit v5 on v4

--- a/solution.py
+++ b/solution.py
@@ -118,17 +118,18 @@
     half = block_size // 2
     half_peers = peers // 2
     kept = started(arrived_ref, held_ref, sem)
+    row_order = sorted(range(peers), key=lambda peer: places[peer])
+
     adam_sq = jnp.zeros((8, block_size), F32)
     shampoo_sq = jnp.zeros((8, block_size), F32)
     for slot in range(slots):
-        for peer in range(peers):
+        for peer in row_order:
             rows = rows_of(places[peer], piece_rows)
             held = arrived_ref[peer, slot]
             low_ref[slot, rows, :] = held.astype(BF16)
             new_second = 0.99 * second_ref[slot, rows, :] + 0.01 * held * held
-            adam = held / (jnp.sqrt(new_second) + 1e-08)
+            adam = held * pl.reciprocal(jnp.sqrt(new_second) + 1e-08)
             adam_sq += sum_rows(adam * adam)
-    for slot in range(slots):
         for part in range(2):
             rows = slice(part * half, (part + 1) * half)
             left_applied = jnp.dot(
@@ -139,9 +140,9 @@
                 half_peers, piece_rows, block_size
             )
             shampoo_sq += sum_rows(shampoo * shampoo)
-    ranks = sums_ref.shape[0]
-    sums_ref[:, 0, :] = jnp.full((ranks, 128), jnp.sum(adam_sq), F32)
-    sums_ref[:, 1, :] = jnp.full((ranks, 128), jnp.sum(shampoo_sq), F32)
+    first = lax.broadcasted_iota(jnp.int32, (2, 128), 0) == 0
+    sums = jnp.where(first, jnp.sum(adam_sq), jnp.sum(shampoo_sq))
+    sums_ref[...] = jnp.broadcast_to(sums[None], sums_ref.shape)
     kept.wait()
 
 

time: 93 us -> 93 us (level)
  no operation moved by 1% of the time
where the time goes in v5:
time: 93 us; the launch traced here: 92.8 us
  blocking collectives  50.8 us (55%)
  waiting for transfers between devices  19.6 us (21%)
  Pallas kernels  16.8 us (18%)
  starting transfers between devices  4.95 us (5%)
    all_to_all x1, blocking collectives, body(): arrived = exchange(outgoing, OUT_ORDER)  32.5 us
    all_to_all x1, waiting for transfers between devices, body(): returned = exchange(step, BACK_ORDER)  19.6 us
    all_to_all x1, blocking collectives, body(): sums = exchange(sums, DP + TENSOR)  18.3 us
    pallas_call x1, Pallas kernels, body(): pl.pallas_call(functools.partial(rest_kernel, out_places, back_places), o...  9.1 us
    all_to_all x1, starting transfers between devices, body(): returned = exchange(step, BACK_ORDER)  4.95 us
    pallas_call x1, Pallas kernels, body(): pl.pallas_call(functools.partial(mid_kernel, out_places), out_shape=(vmem...  2.5 us
    pallas_call x1, Pallas kernels, body(): pl.pallas_call(functools.partial(unpack_kernel, back_places), out_shape=h...  1.96 us
  transfers between devices with their start and end apart: 1, of which 1 were waited for; matrix products, arithmetic and copies ran while one was open for 0% of the time, Pallas kernels for 10%

profile of v5, /device:TPU:9, one launch (start us, length us, event | category | flops | bytes accessed | tf_op | source)
XLA Modules:
  0.0 92.8 jit_solution(617320198837017231)
XLA Ops:
  0.6 1.6 %pack.1 = f32[16,2,32,512]{3,2,1,0:T(8,128)S(1)} custom-call(s32[1,32]{1,0:T(1,128)} %order_ref.3, f32[512,1024]{1,0:T(8,128)} %grad_ref.1), custom_call_target="tpu_custom_call" | custom-call | tf_op jit(solution)/shard_map/pack/pallas_call | solution.py:245
  2.3 0.0 copy-start
  2.3 0.0 copy-start.2
  2.3 0.0 copy-start.3
  2.3 32.5 %all_to_all.15.arrived_ref = f32[16,2,32,512]{3,2,1,0:T(8,128)S(1)} all-to-all(f32[16,2,32,512]{3,2,1,0:T(8,128)S(1)} %pack.1), channel_id=1, replica_groups=mesh['z'=4,'yh'=2,'x'=4,'yl'=2,'core'=2] {'x','yl','core'}, dimensions={0} | all-to-all | bytes 4194304 | tf_op jit(solution)/shard_map/all_to_all | solution.py:257
  34.7 0.0 copy-done
  34.7 0.0 copy-done.2
  34.7 0.0 copy-done.3
  34.8 0.0 copy-start.1
  34.8 2.5 %mid.1 = (f32[16,2,32,512]{3,2,1,0:T(8,128)S(1)}, f32[16,2,32,512]{3,2,1,0:T(8,128)}, f32[128,2,128]{2,1,0:T(2,128)S(1)}) custom-call(f32[16,2,32,512]{3,2,1,0:T(8,128)S(1)} %all_to_all.15.arrived_ref, f32[2,512,512]{2,1,0:T(8,128)S(1)} %copy-done, bf16[2,512,512]{2,1,0:T(8,128)(2,1)S(1)} %copy-done.2, bf16[2,512,512]{2,1,0:T(8,128)(2,1)S(1)} %copy-done.3), custom_call_target="tpu_custom_call" | custom-call | tf_op jit(solution)/shard_map/mid/pallas_call | solution.py:259
  37.3 18.3 %all_to_all.16.sums_ref = f32[128,2,128]{2,1,0:T(2,128)S(1)} all-to-all(f32[128,2,128]{2,1,0:T(2,128)S(1)} %get-tuple-element.13), channel_id=1, replica_groups=mesh['z'=4,'yh'=2,'x'=4,'yl'=2,'core'=2] {'z','yh','x','yl','core'}, dimensions={0} | all-to-all | bytes 262144 | tf_op jit(solution)/shard_map/all_to_all | solution.py:268
  55.6 0.0 copy-done.1
  55.6 1.6 %step.1.step_ref = f32[16,2,32,512]{3,2,1,0:T(8,128)} custom-call(f32[128,2,128]{2,1,0:T(2,128)S(1)} %all_to_all.16.sums_ref, f32[16,2,32,512]{3,2,1,0:T(8,128)S(1)} %get-tuple-element.14.shampoo_ref, f32[2,512,512]{2,1,0:T(8,128)S(1)} %copy-done.1), custom_call_target="tpu_custom_call" | custom-call | tf_op jit(solution)/shard_map/step/pallas_call | solution.py:270
  57.2 5.0 %all-to-all-start.2 = ((f32[16,2,32,512]{3,2,1,0:T(8,128)}), f32[16,2,32,512]{3,2,1,0:T(8,128)S(1)}, u32[]{:S(2)}, u32[]{:S(2)}) async-start(f32[16,2,32,512]{3,2,1,0:T(8,128)} %step.1.step_ref), calls=%async_computation.2 | async-start | bytes 4194304 | tf_op jit(solution)/shard_map/all_to_all | solution.py:279
  62.1 9.1 %rest.1 = (f32[2,512,512]{2,1,0:T(8,128)}, f32[2,512,512]{2,1,0:T(8,128)}, f32[2,512,512]{2,1,0:T(8,128)}, f32[2,512,512]{2,1,0:T(8,128)}) custom-call(f32[16,2,32,512]{3,2,1,0:T(8,128)} %get-tuple-element.12.held_ref, f32[2,512,512]{2,1,0:T(8,128)} %second_ref.3, f32[2,512,512]{2,1,0:T(8,128)} %left_ref.3, f32[2,512,512]{2,1,0:T(8,128)} %right_ref.3, ...), custom_call_target="tpu_custom_call" | custom-call | flops 3221225472 | bytes 18874368 | tf_op jit(solution)/shard_map/rest/pallas_call | solution.py:281
  71.2 19.6 %all-to-all-done.2.moved_ref = f32[16,2,32,512]{3,2,1,0:T(8,128)S(1)} async-done(((f32[16,2,32,512]{3,2,1,0:T(8,128)}), f32[16,2,32,512]{3,2,1,0:T(8,128)S(1)}, u32[]{:S(2)}, u32[]{:S(2)}) %all-to-all-start.2) | async-done | bytes 2097184 | tf_op jit(solution)/shard_map/all_to_all | solution.py:279
  90.8 2.0 %unpack.1 = f32[512,1024]{1,0:T(8,128)} custom-call(s32[1,32]{1,0:T(1,128)} %order_ref.3, f32[16,2,32,512]{3,2,1,0:T(8,128)S(1)} %all-to-all-done.2.moved_ref), custom_call_target="tpu_custom_call" | custom-call | tf_op jit(solution)/shard_map/unpack/pallas_call | solution.py:298
Async XLA Ops:
  2.3 32.5 %copy-start = (f32[2,512,512]{2,1,0:T(8,128)S(1)}, f32[2,512,512]{2,1,0:T(8,128)}, u32[]{:S(2)}) copy-start(f32[2,512,512]{2,1,0:T(8,128)} %second_ref.3) | copy-start | bytes 6291460
  2.3 32.5 %copy-start.2 = (bf16[2,512,512]{2,1,0:T(8,128)(2,1)S(1)}, bf16[2,512,512]{2,1,0:T(8,128)(2,1)}, u32[]{:S(2)}) copy-start(bf16[2,512,512]{2,1,0:T(8,128)(2,1)} %left_ref.2) | copy-start | bytes 3145732
  2.3 32.5 %copy-start.3 = (bf16[2,512,512]{2,1,0:T(8,128)(2,1)S(1)}, bf16[2,512,512]{2,1,0:T(8,128)(2,1)}, u32[]{:S(2)}) copy-start(bf16[2,512,512]{2,1,0:T(8,128)(2,1)} %right_ref.2) | copy-start | bytes 3145732
  34.8 20.8 %copy-start.1 = (f32[2,512,512]{2,1,0:T(8,128)S(1)}, f32[2,512,512]{2,1,0:T(8,128)}, u32[]{:S(2)}) copy-start(f32[2,512,512]{2,1,0:T(8,128)} %momentum_ref.3) | copy-start | bytes 6291460
  57.2 33.6 %all-to-all-start.2 = ((f32[16,2,32,512]{3,2,1,0:T(8,128)}), f32[16,2,32,512]{3,2,1,0:T(8,128)S(1)}, u32[]{:S(2)}, u32[]{:S(2)}) async-start(f32[16,2,32,512]{3,2,1,0:T(8,128)} %step.1.step_ref), calls=%async_computation.2 | async-start | bytes 4194304 | tf_op jit(solution)/shard_map/all_to_all | solution.py:279

commit v6 on v5

--- a/solution.py
+++ b/solution.py
@@ -112,7 +112,8 @@
 
 
 def mid_kernel(
-    places, arrived_ref, second_ref, left_ref, right_ref, shampoo_ref, held_ref, sums_ref, low_ref, sem
+    places, arrived_ref, second_ref, left_ref, right_ref, shampoo_ref, held_ref, sums_ref,
+    low_ref, applied_ref, sem,
 ):
     peers, slots, piece_rows, block_size = arrived_ref.shape
     half = block_size // 2
@@ -130,12 +131,18 @@
             new_second = 0.99 * second_ref[slot, rows, :] + 0.01 * held * held
             adam = held * pl.reciprocal(jnp.sqrt(new_second) + 1e-08)
             adam_sq += sum_rows(adam * adam)
+    for slot in range(slots):
         for part in range(2):
             rows = slice(part * half, (part + 1) * half)
-            left_applied = jnp.dot(
+            applied_ref[slot, rows, :] = jnp.dot(
                 left_ref[slot, rows, :], low_ref[slot], preferred_element_type=F32
             ).astype(BF16)
-            shampoo = jnp.dot(left_applied, right_ref[slot], preferred_element_type=F32)
+    for slot in range(slots):
+        for part in range(2):
+            rows = slice(part * half, (part + 1) * half)
+            shampoo = jnp.dot(
+                applied_ref[slot, rows, :], right_ref[slot], preferred_element_type=F32
+            )
             shampoo_ref[part * half_peers : (part + 1) * half_peers, slot] = shampoo.reshape(
                 half_peers, piece_rows, block_size
             )
@@ -174,8 +181,8 @@
     sems, store_sem,
 ):
     peers, slots, piece_rows, block_size = held_ref.shape
-    loads = []
-    for slot in range(slots):
+
+    def load(slot):
         pairs = (
             (left_ref.at[slot], left_here.at[slot]),
             (right_ref.at[slot], right_here.at[slot]),
@@ -184,9 +191,11 @@
             (step_ref.at[:, slot], step_here.at[:, slot]),
             (held_ref.at[:, slot], held_here.at[:, slot]),
         )[::-1]
-        loads.append([started(*pair, sems.at[slot, k]) for k, pair in enumerate(pairs)])
+        return [started(*pair, sems.at[slot, k]) for k, pair in enumerate(pairs)]
+
     scale = 0.1 / block_size
     half = block_size // 2
+    loads = [load(0)]
     for slot in range(slots):
         loads[slot][0].wait()
         for peer in range(peers):
@@ -214,8 +223,10 @@
                 )
                 here[slot, cut, :] = 0.9 * here[slot, cut, :] + scale * gram
             started(here.at[slot], ref.at[slot], store_sem)
-        for load in loads[slot][1:4]:
-            load.wait()
+        if slot + 1 < slots:
+            loads.append(load(slot + 1))
+        for pending in loads[slot][1:4]:
+            pending.wait()
         for peer in range(peers):
             rows = rows_of(out_places[peer], piece_rows)
             held = held_here[peer, slot]
@@ -261,7 +272,7 @@
         out_shape=(vmem(pair), hbm(pair), jax.ShapeDtypeStruct((ranks, 2, 128), F32)),
         in_specs=[VMEM] * 4,
         out_specs=(VMEM, ANY, VMEM),
-        scratch_shapes=[vmem(blocks, BF16), DMA],
+        scratch_shapes=[vmem(blocks, BF16), vmem(blocks, BF16), DMA],
         compiler_params=params(16),
         name="mid",
     )(in_vmem(arrived), in_vmem(second), in_vmem(left_root), in_vmem(right_root))

time: 93 us -> 92.8 us (level)
  waiting for transfers between devices: 19.6 us -> 16.5 us
  Pallas kernels: 16.8 us -> 19.5 us
    all_to_all x1, waiting for transfers between devices: 19.6 us -> 16.5 us  [body(): returned = exchange(step, BACK_ORDER)]
    pallas_call x1, Pallas kernels: 9.1 us -> 12.1 us  [body(): pl.pallas_call(functools.partial(rest_kernel, out_places, back_places), o...]
  transfers between devices with their start and end apart: 1 -> 1, of which waited for: 1 -> 1; matrix products, arithmetic and copies ran while one was open for 0% -> 0% of each run, Pallas kernels for 10% -> 13%
where the time goes in v6:
time: 92.8 us; the launch traced here: 92.5 us
  blocking collectives  50.8 us (55%)
  Pallas kernels  19.5 us (21%)
  waiting for transfers between devices  16.5 us (18%)
  starting transfers between devices  4.95 us (5%)
    all_to_all x1, blocking collectives, body(): arrived = exchange(outgoing, OUT_ORDER)  32.5 us
    all_to_all x1, blocking collectives, body(): sums = exchange(sums, DP + TENSOR)  18.3 us
    all_to_all x1, waiting for transfers between devices, body(): returned = exchange(step, BACK_ORDER)  16.5 us
    pallas_call x1, Pallas kernels, body(): pl.pallas_call(functools.partial(rest_kernel, out_places, back_places), o...  12.1 us
    all_to_all x1, starting transfers between devices, body(): returned = exchange(step, BACK_ORDER)  4.95 us
    pallas_call x1, Pallas kernels, body(): pl.pallas_call(functools.partial(mid_kernel, out_places), out_shape=(vmem...  2.23 us
    pallas_call x1, Pallas kernels, body(): pl.pallas_call(functools.partial(unpack_kernel, back_places), out_shape=h...  1.96 us
  transfers between devices with their start and end apart: 1, of which 1 were waited for; matrix products, arithmetic and copies ran while one was open for 0% of the time, Pallas kernels for 13%

profile of v6, /device:TPU:9, one launch (start us, length us, event | category | flops | bytes accessed | tf_op | source)
XLA Modules:
  0.0 92.5 jit_solution(13870786379606999673)
XLA Ops:
  0.6 1.6 %pack.1 = f32[16,2,32,512]{3,2,1,0:T(8,128)S(1)} custom-call(s32[1,32]{1,0:T(1,128)} %order_ref.3, f32[512,1024]{1,0:T(8,128)} %grad_ref.1), custom_call_target="tpu_custom_call" | custom-call | tf_op jit(solution)/shard_map/pack/pallas_call | solution.py:256
  2.3 0.0 copy-start
  2.3 0.0 copy-start.2
  2.3 0.0 copy-start.3
  2.3 32.5 %all_to_all.15.arrived_ref = f32[16,2,32,512]{3,2,1,0:T(8,128)S(1)} all-to-all(f32[16,2,32,512]{3,2,1,0:T(8,128)S(1)} %pack.1), channel_id=1, replica_groups=mesh['z'=4,'yh'=2,'x'=4,'yl'=2,'core'=2] {'x','yl','core'}, dimensions={0} | all-to-all | bytes 4194304 | tf_op jit(solution)/shard_map/all_to_all | solution.py:268
  34.7 0.0 copy-done
  34.7 0.0 copy-done.2
  34.7 0.0 copy-done.3
  34.8 0.0 copy-start.1
  34.8 2.2 %mid.1 = (f32[16,2,32,512]{3,2,1,0:T(8,128)S(1)}, f32[16,2,32,512]{3,2,1,0:T(8,128)}, f32[128,2,128]{2,1,0:T(2,128)S(1)}) custom-call(f32[16,2,32,512]{3,2,1,0:T(8,128)S(1)} %all_to_all.15.arrived_ref, f32[2,512,512]{2,1,0:T(8,128)S(1)} %copy-done, bf16[2,512,512]{2,1,0:T(8,128)(2,1)S(1)} %copy-done.2, bf16[2,512,512]{2,1,0:T(8,128)(2,1)S(1)} %copy-done.3), custom_call_target="tpu_custom_call" | custom-call | tf_op jit(solution)/shard_map/mid/pallas_call | solution.py:270
  37.0 18.3 %all_to_all.16.sums_ref = f32[128,2,128]{2,1,0:T(2,128)S(1)} all-to-all(f32[128,2,128]{2,1,0:T(2,128)S(1)} %get-tuple-element.13), channel_id=1, replica_groups=mesh['z'=4,'yh'=2,'x'=4,'yl'=2,'core'=2] {'z','yh','x','yl','core'}, dimensions={0} | all-to-all | bytes 262144 | tf_op jit(solution)/shard_map/all_to_all | solution.py:279
  55.3 0.0 copy-done.1
  55.3 1.6 %step.1.step_ref = f32[16,2,32,512]{3,2,1,0:T(8,128)} custom-call(f32[128,2,128]{2,1,0:T(2,128)S(1)} %all_to_all.16.sums_ref, f32[16,2,32,512]{3,2,1,0:T(8,128)S(1)} %get-tuple-element.14.shampoo_ref, f32[2,512,512]{2,1,0:T(8,128)S(1)} %copy-done.1), custom_call_target="tpu_custom_call" | custom-call | tf_op jit(solution)/shard_map/step/pallas_call | solution.py:281
  56.9 5.0 %all-to-all-start.2 = ((f32[16,2,32,512]{3,2,1,0:T(8,128)}), f32[16,2,32,512]{3,2,1,0:T(8,128)S(1)}, u32[]{:S(2)}, u32[]{:S(2)}) async-start(f32[16,2,32,512]{3,2,1,0:T(8,128)} %step.1.step_ref), calls=%async_computation.2 | async-start | bytes 4194304 | tf_op jit(solution)/shard_map/all_to_all | solution.py:290
  61.9 12.1 %rest.1 = (f32[2,512,512]{2,1,0:T(8,128)}, f32[2,512,512]{2,1,0:T(8,128)}, f32[2,512,512]{2,1,0:T(8,128)}, f32[2,512,512]{2,1,0:T(8,128)}) custom-call(f32[16,2,32,512]{3,2,1,0:T(8,128)} %get-tuple-element.12.held_ref, f32[2,512,512]{2,1,0:T(8,128)} %second_ref.3, f32[2,512,512]{2,1,0:T(8,128)} %left_ref.3, f32[2,512,512]{2,1,0:T(8,128)} %right_ref.3, ...), custom_call_target="tpu_custom_call" | custom-call | flops 3221225472 | bytes 18874368 | tf_op jit(solution)/shard_map/rest/pallas_call | solution.py:292
  74.0 16.5 %all-to-all-done.2.moved_ref = f32[16,2,32,512]{3,2,1,0:T(8,128)S(1)} async-done(((f32[16,2,32,512]{3,2,1,0:T(8,128)}), f32[16,2,32,512]{3,2,1,0:T(8,128)S(1)}, u32[]{:S(2)}, u32[]{:S(2)}) %all-to-all-start.2) | async-done | bytes 2097184 | tf_op jit(solution)/shard_map/all_to_all | solution.py:290
  90.6 2.0 %unpack.1 = f32[512,1024]{1,0:T(8,128)} custom-call(s32[1,32]{1,0:T(1,128)} %order_ref.3, f32[16,2,32,512]{3,2,1,0:T(8,128)S(1)} %all-to-all-done.2.moved_ref), custom_call_target="tpu_custom_call" | custom-call | tf_op jit(solution)/shard_map/unpack/pallas_call | solution.py:309
Async XLA Ops:
  2.3 32.5 %copy-start = (f32[2,512,512]{2,1,0:T(8,128)S(1)}, f32[2,512,512]{2,1,0:T(8,128)}, u32[]{:S(2)}) copy-start(f32[2,512,512]{2,1,0:T(8,128)} %second_ref.3) | copy-start | bytes 6291460
  2.3 32.5 %copy-start.2 = (bf16[2,512,512]{2,1,0:T(8,128)(2,1)S(1)}, bf16[2,512,512]{2,1,0:T(8,128)(2,1)}, u32[]{:S(2)}) copy-start(bf16[2,512,512]{2,1,0:T(8,128)(2,1)} %left_ref.2) | copy-start | bytes 3145732
  2.3 32.5 %copy-start.3 = (bf16[2,512,512]{2,1,0:T(8,128)(2,1)S(1)}, bf16[2,512,512]{2,1,0:T(8,128)(2,1)}, u32[]{:S(2)}) copy-start(bf16[2,512,512]{2,1,0:T(8,128)(2,1)} %right_ref.2) | copy-start | bytes 3145732
  34.8 20.6 %copy-start.1 = (f32[2,512,512]{2,1,0:T(8,128)S(1)}, f32[2,512,512]{2,1,0:T(8,128)}, u32[]{:S(2)}) copy-start(f32[2,512,512]{2,1,0:T(8,128)} %momentum_ref.3) | copy-start | bytes 6291460
  56.9 33.6 %all-to-all-start.2 = ((f32[16,2,32,512]{3,2,1,0:T(8,128)}), f32[16,2,32,512]{3,2,1,0:T(8,128)S(1)}, u32[]{:S(2)}, u32[]{:S(2)}) async-start(f32[16,2,32,512]{3,2,1,0:T(8,128)} %step.1.step_ref), calls=%async_computation.2 | async-start | bytes 4194304 | tf_op jit(solution)/shard_map/all_to_all | solution.py:290

commit v7 on v6

--- a/solution.py
+++ b/solution.py
@@ -60,15 +60,14 @@
     copy(ref, ref, sem).wait()
 
 
-def piece_of(ref, block, piece_rows, block_size):
-    col_blocks = ref.shape[1] // block_size
-    row = pl.multiple_of((block // col_blocks) * piece_rows, piece_rows)
-    col = pl.multiple_of((block % col_blocks) * block_size, block_size)
-    return ref.at[pl.ds(row, piece_rows), pl.ds(col, block_size)]
-
-
 def rows_of(peer, piece_rows):
     return slice(peer * piece_rows, (peer + 1) * piece_rows)
+
+
+def put_index(places, slots, order_ref, index_ref):
+    for peer, place in enumerate(places):
+        for slot in range(slots):
+            index_ref[order_ref[0, place * slots + slot]] = peer * slots + slot
 
 
 def pack_kernel(
@@ -83,9 +82,7 @@
         rows = pl.ds(chunk * chunk_rows, chunk_rows)
         loads.append(started(grad_ref.at[rows], here_ref.at[rows], sems.at[chunk]))
     table.wait()
-    for peer in range(peers):
-        for slot in range(slots):
-            index_ref[order_here[0, places[peer] * slots + slot]] = peer * slots + slot
+    put_index(places, slots, order_here, index_ref)
     for chunk, load in enumerate(loads):
         load.wait()
         for row in range(chunk * chunk_rows, (chunk + 1) * chunk_rows, piece_rows):
@@ -96,15 +93,21 @@
                 ]
 
 
-def unpack_kernel(places, order_ref, moved_ref, out_ref, sem):
+def unpack_kernel(places, order_ref, moved_ref, out_ref, here_ref, index_ref, sem):
     peers, slots, piece_rows, block_size = moved_ref.shape
-    for peer in range(peers):
-        for slot in range(slots):
-            block = order_ref[0, places[peer] * slots + slot]
-            started(
-                moved_ref.at[peer, slot], piece_of(out_ref, block, piece_rows, block_size), sem
-            )
-    wait_all(moved_ref, sem)
+    put_index(places, slots, order_ref, index_ref)
+    col_blocks = out_ref.shape[1] // block_size
+    chunk_rows = out_ref.shape[0] // (2 * CHUNKS)
+    for start in range(0, out_ref.shape[0], chunk_rows):
+        for row in range(start, start + chunk_rows, piece_rows):
+            for column in range(col_blocks):
+                at = index_ref[row // piece_rows * col_blocks + column]
+                here_ref[
+                    row : row + piece_rows, column * block_size : (column + 1) * block_size
+                ] = moved_ref[at // slots, at % slots]
+        rows = pl.ds(start, chunk_rows)
+        started(here_ref.at[rows], out_ref.at[rows], sem)
+    wait_all(here_ref, sem)
 
 
 def sum_rows(x):
@@ -126,17 +129,19 @@
     for slot in range(slots):
         for peer in row_order:
             rows = rows_of(places[peer], piece_rows)
-            held = arrived_ref[peer, slot]
-            low_ref[slot, rows, :] = held.astype(BF16)
-            new_second = 0.99 * second_ref[slot, rows, :] + 0.01 * held * held
-            adam = held * pl.reciprocal(jnp.sqrt(new_second) + 1e-08)
-            adam_sq += sum_rows(adam * adam)
+            low_ref[slot, rows, :] = arrived_ref[peer, slot].astype(BF16)
     for slot in range(slots):
         for part in range(2):
             rows = slice(part * half, (part + 1) * half)
             applied_ref[slot, rows, :] = jnp.dot(
                 left_ref[slot, rows, :], low_ref[slot], preferred_element_type=F32
             ).astype(BF16)
+            for peer in row_order[part * half_peers : (part + 1) * half_peers]:
+                rows = rows_of(places[peer], piece_rows)
+                held = arrived_ref[peer, slot]
+                new_second = 0.99 * second_ref[slot, rows, :] + 0.01 * held * held
+                adam = held * pl.reciprocal(jnp.sqrt(new_second) + 1e-08)
+                adam_sq += sum_rows(adam * adam)
     for slot in range(slots):
         for part in range(2):
             rows = slice(part * half, (part + 1) * half)
@@ -311,7 +316,7 @@
         out_shape=hbm(grad.shape),
         in_specs=[pl.BlockSpec(memory_space=pltpu.SMEM), VMEM],
         out_specs=ANY,
-        scratch_shapes=[DMA],
+        scratch_shapes=[vmem(grad.shape), pltpu.SMEM((peers * slots,), jnp.int32), DMA],
         compiler_params=params(8),
         name="unpack",
     )(order, in_vmem(returned))

time: 92.8 us -> 93.1 us (level)
  no operation moved by 1% of the time
where the time goes in v7:
time: 93.1 us; the launch traced here: 92.9 us
  blocking collectives  50.8 us (55%)
  Pallas kernels  19.9 us (21%)
  waiting for transfers between devices  16.5 us (18%)
  starting transfers between devices  4.95 us (5%)
    all_to_all x1, blocking collectives, body(): arrived = exchange(outgoing, OUT_ORDER)  32.5 us
    all_to_all x1, blocking collectives, body(): sums = exchange(sums, DP + TENSOR)  18.3 us
    all_to_all x1, waiting for transfers between devices, body(): returned = exchange(step, BACK_ORDER)  16.5 us
    pallas_call x1, Pallas kernels, body(): pl.pallas_call(functools.partial(rest_kernel, out_places, back_places), o...  12.1 us
    all_to_all x1, starting transfers between devices, body(): returned = exchange(step, BACK_ORDER)  4.95 us
    pallas_call x1, Pallas kernels, body(): pl.pallas_call(functools.partial(mid_kernel, out_places), out_shape=(vmem...  2.52 us
    pallas_call x1, Pallas kernels, body(): pl.pallas_call(functools.partial(unpack_kernel, back_places), out_shape=h...  2.04 us
  transfers between devices with their start and end apart: 1, of which 1 were waited for; matrix products, arithmetic and copies ran while one was open for 0% of the time, Pallas kernels for 13%

profile of v7, /device:TPU:9, one launch (start us, length us, event | category | flops | bytes accessed | tf_op | source)
XLA Modules:
  0.0 92.9 jit_solution(16026550675850555334)
XLA Ops:
  0.6 1.6 %pack.1 = f32[16,2,32,512]{3,2,1,0:T(8,128)S(1)} custom-call(s32[1,32]{1,0:T(1,128)} %order_ref.3, f32[512,1024]{1,0:T(8,128)} %grad_ref.1), custom_call_target="tpu_custom_call" | custom-call | tf_op jit(solution)/shard_map/pack/pallas_call | solution.py:261
  2.3 0.0 copy-start
  2.3 0.0 copy-start.2
  2.3 0.0 copy-start.3
  2.3 32.5 %all_to_all.15.arrived_ref = f32[16,2,32,512]{3,2,1,0:T(8,128)S(1)} all-to-all(f32[16,2,32,512]{3,2,1,0:T(8,128)S(1)} %pack.1), channel_id=1, replica_groups=mesh['z'=4,'yh'=2,'x'=4,'yl'=2,'core'=2] {'x','yl','core'}, dimensions={0} | all-to-all | bytes 4194304 | tf_op jit(solution)/shard_map/all_to_all | solution.py:273
  34.7 0.0 copy-done
  34.7 0.0 copy-done.2
  34.7 0.0 copy-done.3
  34.8 0.0 copy-start.1
  34.8 2.5 %mid.1 = (f32[16,2,32,512]{3,2,1,0:T(8,128)S(1)}, f32[16,2,32,512]{3,2,1,0:T(8,128)}, f32[128,2,128]{2,1,0:T(2,128)S(1)}) custom-call(f32[16,2,32,512]{3,2,1,0:T(8,128)S(1)} %all_to_all.15.arrived_ref, f32[2,512,512]{2,1,0:T(8,128)S(1)} %copy-done, bf16[2,512,512]{2,1,0:T(8,128)(2,1)S(1)} %copy-done.2, bf16[2,512,512]{2,1,0:T(8,128)(2,1)S(1)} %copy-done.3), custom_call_target="tpu_custom_call" | custom-call | tf_op jit(solution)/shard_map/mid/pallas_call | solution.py:275
  37.3 18.3 %all_to_all.16.sums_ref = f32[128,2,128]{2,1,0:T(2,128)S(1)} all-to-all(f32[128,2,128]{2,1,0:T(2,128)S(1)} %get-tuple-element.13), channel_id=1, replica_groups=mesh['z'=4,'yh'=2,'x'=4,'yl'=2,'core'=2] {'z','yh','x','yl','core'}, dimensions={0} | all-to-all | bytes 262144 | tf_op jit(solution)/shard_map/all_to_all | solution.py:284
  55.6 0.0 copy-done.1
  55.6 1.6 %step.1.step_ref = f32[16,2,32,512]{3,2,1,0:T(8,128)} custom-call(f32[128,2,128]{2,1,0:T(2,128)S(1)} %all_to_all.16.sums_ref, f32[16,2,32,512]{3,2,1,0:T(8,128)S(1)} %get-tuple-element.14.shampoo_ref, f32[2,512,512]{2,1,0:T(8,128)S(1)} %copy-done.1), custom_call_target="tpu_custom_call" | custom-call | tf_op jit(solution)/shard_map/step/pallas_call | solution.py:286
  57.2 5.0 %all-to-all-start.2 = ((f32[16,2,32,512]{3,2,1,0:T(8,128)}), f32[16,2,32,512]{3,2,1,0:T(8,128)S(1)}, u32[]{:S(2)}, u32[]{:S(2)}) async-start(f32[16,2,32,512]{3,2,1,0:T(8,128)} %step.1.step_ref), calls=%async_computation.2 | async-start | bytes 4194304 | tf_op jit(solution)/shard_map/all_to_all | solution.py:295
  62.2 12.1 %rest.1 = (f32[2,512,512]{2,1,0:T(8,128)}, f32[2,512,512]{2,1,0:T(8,128)}, f32[2,512,512]{2,1,0:T(8,128)}, f32[2,512,512]{2,1,0:T(8,128)}) custom-call(f32[16,2,32,512]{3,2,1,0:T(8,128)} %get-tuple-element.12.held_ref, f32[2,512,512]{2,1,0:T(8,128)} %second_ref.3, f32[2,512,512]{2,1,0:T(8,128)} %left_ref.3, f32[2,512,512]{2,1,0:T(8,128)} %right_ref.3, ...), custom_call_target="tpu_custom_call" | custom-call | flops 3221225472 | bytes 18874368 | tf_op jit(solution)/shard_map/rest/pallas_call | solution.py:297
  74.3 16.5 %all-to-all-done.2.moved_ref = f32[16,2,32,512]{3,2,1,0:T(8,128)S(1)} async-done(((f32[16,2,32,512]{3,2,1,0:T(8,128)}), f32[16,2,32,512]{3,2,1,0:T(8,128)S(1)}, u32[]{:S(2)}, u32[]{:S(2)}) %all-to-all-start.2) | async-done | bytes 2097184 | tf_op jit(solution)/shard_map/all_to_all | solution.py:295
  90.8 2.0 %unpack.1 = f32[512,1024]{1,0:T(8,128)} custom-call(s32[1,32]{1,0:T(1,128)} %order_ref.3, f32[16,2,32,512]{3,2,1,0:T(8,128)S(1)} %all-to-all-done.2.moved_ref), custom_call_target="tpu_custom_call" | custom-call | tf_op jit(solution)/shard_map/unpack/pallas_call | solution.py:314
Async XLA Ops:
  2.3 32.5 %copy-start = (f32[2,512,512]{2,1,0:T(8,128)S(1)}, f32[2,512,512]{2,1,0:T(8,128)}, u32[]{:S(2)}) copy-start(f32[2,512,512]{2,1,0:T(8,128)} %second_ref.3) | copy-start | bytes 6291460
  2.3 32.5 %copy-start.2 = (bf16[2,512,512]{2,1,0:T(8,128)(2,1)S(1)}, bf16[2,512,512]{2,1,0:T(8,128)(2,1)}, u32[]{:S(2)}) copy-start(bf16[2,512,512]{2,1,0:T(8,128)(2,1)} %left_ref.2) | copy-start | bytes 3145732
  2.3 32.5 %copy-start.3 = (bf16[2,512,512]{2,1,0:T(8,128)(2,1)S(1)}, bf16[2,512,512]{2,1,0:T(8,128)(2,1)}, u32[]{:S(2)}) copy-start(bf16[2,512,512]{2,1,0:T(8,128)(2,1)} %right_ref.2) | copy-start | bytes 3145732
  34.8 20.9 %copy-start.1 = (f32[2,512,512]{2,1,0:T(8,128)S(1)}, f32[2,512,512]{2,1,0:T(8,128)}, u32[]{:S(2)}) copy-start(f32[2,512,512]{2,1,0:T(8,128)} %momentum_ref.3) | copy-start | bytes 6291460
  57.2 33.6 %all-to-all-start.2 = ((f32[16,2,32,512]{3,2,1,0:T(8,128)}), f32[16,2,32,512]{3,2,1,0:T(8,128)S(1)}, u32[]{:S(2)}, u32[]{:S(2)}) async-start(f32[16,2,32,512]{3,2,1,0:T(8,128)} %step.1.step_ref), calls=%async_computation.2 | async-start | bytes 4194304 | tf_op jit(solution)/shard_map/all_to_all | solution.py:295

commit v8 on v6

--- a/solution.py
+++ b/solution.py
@@ -116,8 +116,6 @@
     low_ref, applied_ref, sem,
 ):
     peers, slots, piece_rows, block_size = arrived_ref.shape
-    half = block_size // 2
-    half_peers = peers // 2
     kept = started(arrived_ref, held_ref, sem)
     row_order = sorted(range(peers), key=lambda peer: places[peer])
 
@@ -132,21 +130,13 @@
             adam = held * pl.reciprocal(jnp.sqrt(new_second) + 1e-08)
             adam_sq += sum_rows(adam * adam)
     for slot in range(slots):
-        for part in range(2):
-            rows = slice(part * half, (part + 1) * half)
-            applied_ref[slot, rows, :] = jnp.dot(
-                left_ref[slot, rows, :], low_ref[slot], preferred_element_type=F32
-            ).astype(BF16)
+        applied_ref[slot] = jnp.dot(
+            left_ref[slot], low_ref[slot], preferred_element_type=F32
+        ).astype(BF16)
     for slot in range(slots):
-        for part in range(2):
-            rows = slice(part * half, (part + 1) * half)
-            shampoo = jnp.dot(
-                applied_ref[slot, rows, :], right_ref[slot], preferred_element_type=F32
-            )
-            shampoo_ref[part * half_peers : (part + 1) * half_peers, slot] = shampoo.reshape(
-                half_peers, piece_rows, block_size
-            )
-            shampoo_sq += sum_rows(shampoo * shampoo)
+        shampoo = jnp.dot(applied_ref[slot], right_ref[slot], preferred_element_type=F32)
+        shampoo_ref[:, slot] = shampoo.reshape(peers, piece_rows, block_size)
+        shampoo_sq += sum_rows(shampoo * shampoo)
     first = lax.broadcasted_iota(jnp.int32, (2, 128), 0) == 0
     sums = jnp.where(first, jnp.sum(adam_sq), jnp.sum(shampoo_sq))
     sums_ref[...] = jnp.broadcast_to(sums[None], sums_ref.shape)
@@ -276,7 +266,7 @@
         compiler_params=params(16),
         name="mid",
     )(in_vmem(arrived), in_vmem(second), in_vmem(left_root), in_vmem(right_root))
-    sums = exchange(sums, DP + TENSOR)
+    sums = exchange(sums, (DP + TENSOR)[::-1])
 
     step = pl.pallas_call(
         functools.partial(step_kernel, back_places),

time: 92.8 us -> 92.8 us (level)
  no operation moved by 1% of the time
where the time goes in v8:
time: 92.8 us; the launch traced here: 92.6 us
  blocking collectives  50.7 us (55%)
  Pallas kernels  19.4 us (21%)
  waiting for transfers between devices  16.5 us (18%)
  starting transfers between devices  5.17 us (6%)
    all_to_all x1, blocking collectives, body(): arrived = exchange(outgoing, OUT_ORDER)  32.5 us
    all_to_all x1, blocking collectives, body(): sums = exchange(sums, (DP + TENSOR)[::-1])  18.2 us
    all_to_all x1, waiting for transfers between devices, body(): returned = exchange(step, BACK_ORDER)  16.5 us
    pallas_call x1, Pallas kernels, body(): pl.pallas_call(functools.partial(rest_kernel, out_places, back_places), o...  12.1 us
    all_to_all x1, starting transfers between devices, body(): returned = exchange(step, BACK_ORDER)  5.17 us
    pallas_call x1, Pallas kernels, body(): pl.pallas_call(functools.partial(mid_kernel, out_places), out_shape=(vmem...  2.14 us
    pallas_call x1, Pallas kernels, body(): pl.pallas_call(functools.partial(unpack_kernel, back_places), out_shape=h...  1.96 us
  transfers between devices with their start and end apart: 1, of which 1 were waited for; matrix products, arithmetic and copies ran while one was open for 0% of the time, Pallas kernels for 13%

profile of v8, /device:TPU:9, one launch (start us, length us, event | category | flops | bytes accessed | tf_op | source)
XLA Modules:
  0.0 92.6 jit_solution(5208719137134175504)
XLA Ops:
  0.6 1.6 %pack.1 = f32[16,2,32,512]{3,2,1,0:T(8,128)S(1)} custom-call(s32[1,32]{1,0:T(1,128)} %order_ref.3, f32[512,1024]{1,0:T(8,128)} %grad_ref.1), custom_call_target="tpu_custom_call" | custom-call | tf_op jit(solution)/shard_map/pack/pallas_call | solution.py:246
  2.3 0.0 copy-start
  2.3 0.0 copy-start.2
  2.3 0.0 copy-start.3
  2.3 32.5 %all_to_all.15.arrived_ref = f32[16,2,32,512]{3,2,1,0:T(8,128)S(1)} all-to-all(f32[16,2,32,512]{3,2,1,0:T(8,128)S(1)} %pack.1), channel_id=1, replica_groups=mesh['z'=4,'yh'=2,'x'=4,'yl'=2,'core'=2] {'x','yl','core'}, dimensions={0} | all-to-all | bytes 4194304 | tf_op jit(solution)/shard_map/all_to_all | solution.py:258
  34.7 0.0 copy-done
  34.7 0.0 copy-done.2
  34.7 0.0 copy-done.3
  34.8 0.0 copy-start.1
  34.8 2.1 %mid.1 = (f32[16,2,32,512]{3,2,1,0:T(8,128)S(1)}, f32[16,2,32,512]{3,2,1,0:T(8,128)}, f32[128,2,128]{2,1,0:T(2,128)S(1)}) custom-call(f32[16,2,32,512]{3,2,1,0:T(8,128)S(1)} %all_to_all.15.arrived_ref, f32[2,512,512]{2,1,0:T(8,128)S(1)} %copy-done, bf16[2,512,512]{2,1,0:T(8,128)(2,1)S(1)} %copy-done.2, bf16[2,512,512]{2,1,0:T(8,128)(2,1)S(1)} %copy-done.3), custom_call_target="tpu_custom_call" | custom-call | tf_op jit(solution)/shard_map/mid/pallas_call | solution.py:260
  36.9 18.2 %all_to_all.16.sums_ref = f32[128,2,128]{2,1,0:T(2,128)S(1)} all-to-all(f32[128,2,128]{2,1,0:T(2,128)S(1)} %get-tuple-element.13), channel_id=1, replica_groups=mesh['z'=4,'yh'=2,'x'=4,'yl'=2,'core'=2] {'core','yl','x','yh','z'}, dimensions={0} | all-to-all | bytes 262144 | tf_op jit(solution)/shard_map/all_to_all | solution.py:269
  55.2 0.0 copy-done.1
  55.2 1.6 %step.1.step_ref = f32[16,2,32,512]{3,2,1,0:T(8,128)} custom-call(f32[128,2,128]{2,1,0:T(2,128)S(1)} %all_to_all.16.sums_ref, f32[16,2,32,512]{3,2,1,0:T(8,128)S(1)} %get-tuple-element.14.shampoo_ref, f32[2,512,512]{2,1,0:T(8,128)S(1)} %copy-done.1), custom_call_target="tpu_custom_call" | custom-call | tf_op jit(solution)/shard_map/step/pallas_call | solution.py:271
  56.8 5.2 %all-to-all-start.2 = ((f32[16,2,32,512]{3,2,1,0:T(8,128)}), f32[16,2,32,512]{3,2,1,0:T(8,128)S(1)}, u32[]{:S(2)}, u32[]{:S(2)}) async-start(f32[16,2,32,512]{3,2,1,0:T(8,128)} %step.1.step_ref), calls=%async_computation.2 | async-start | bytes 4194304 | tf_op jit(solution)/shard_map/all_to_all | solution.py:280
  61.9 12.1 %rest.1 = (f32[2,512,512]{2,1,0:T(8,128)}, f32[2,512,512]{2,1,0:T(8,128)}, f32[2,512,512]{2,1,0:T(8,128)}, f32[2,512,512]{2,1,0:T(8,128)}) custom-call(f32[16,2,32,512]{3,2,1,0:T(8,128)} %get-tuple-element.12.held_ref, f32[2,512,512]{2,1,0:T(8,128)} %second_ref.3, f32[2,512,512]{2,1,0:T(8,128)} %left_ref.3, f32[2,512,512]{2,1,0:T(8,128)} %right_ref.3, ...), custom_call_target="tpu_custom_call" | custom-call | flops 3221225472 | bytes 18874368 | tf_op jit(solution)/shard_map/rest/pallas_call | solution.py:282
  74.1 16.5 %all-to-all-done.2.moved_ref = f32[16,2,32,512]{3,2,1,0:T(8,128)S(1)} async-done(((f32[16,2,32,512]{3,2,1,0:T(8,128)}), f32[16,2,32,512]{3,2,1,0:T(8,128)S(1)}, u32[]{:S(2)}, u32[]{:S(2)}) %all-to-all-start.2) | async-done | bytes 2097184 | tf_op jit(solution)/shard_map/all_to_all | solution.py:280
  90.6 2.0 %unpack.1 = f32[512,1024]{1,0:T(8,128)} custom-call(s32[1,32]{1,0:T(1,128)} %order_ref.3, f32[16,2,32,512]{3,2,1,0:T(8,128)S(1)} %all-to-all-done.2.moved_ref), custom_call_target="tpu_custom_call" | custom-call | tf_op jit(solution)/shard_map/unpack/pallas_call | solution.py:299
Async XLA Ops:
  2.3 32.5 %copy-start = (f32[2,512,512]{2,1,0:T(8,128)S(1)}, f32[2,512,512]{2,1,0:T(8,128)}, u32[]{:S(2)}) copy-start(f32[2,512,512]{2,1,0:T(8,128)} %second_ref.3) | copy-start | bytes 6291460
  2.3 32.5 %copy-start.2 = (bf16[2,512,512]{2,1,0:T(8,128)(2,1)S(1)}, bf16[2,512,512]{2,1,0:T(8,128)(2,1)}, u32[]{:S(2)}) copy-start(bf16[2,512,512]{2,1,0:T(8,128)(2,1)} %left_ref.2) | copy-start | bytes 3145732
  2.3 32.5 %copy-start.3 = (bf16[2,512,512]{2,1,0:T(8,128)(2,1)S(1)}, bf16[2,512,512]{2,1,0:T(8,128)(2,1)}, u32[]{:S(2)}) copy-start(bf16[2,512,512]{2,1,0:T(8,128)(2,1)} %right_ref.2) | copy-start | bytes 3145732
  34.8 20.4 %copy-start.1 = (f32[2,512,512]{2,1,0:T(8,128)S(1)}, f32[2,512,512]{2,1,0:T(8,128)}, u32[]{:S(2)}) copy-start(f32[2,512,512]{2,1,0:T(8,128)} %momentum_ref.3) | copy-start | bytes 6291460
  56.8 33.8 %all-to-all-start.2 = ((f32[16,2,32,512]{3,2,1,0:T(8,128)}), f32[16,2,32,512]{3,2,1,0:T(8,128)S(1)}, u32[]{:S(2)}, u32[]{:S(2)}) async-start(f32[16,2,32,512]{3,2,1,0:T(8,128)} %step.1.step_ref), calls=%async_computation.2 | async-start | bytes 4194304 | tf_op jit(solution)/shard_map/all_to_all | solution.py:280

commit v9 on v8

--- a/solution.py
+++ b/solution.py
@@ -17,9 +17,9 @@
 CHUNKS = 4
 
 
-FINE = (("z", 4), ("yh", 2), ("x", 4), ("yl", 2), ("core", 2))
-DP, TENSOR = ("z", "yh"), ("x", "yl", "core")
-OUT_ORDER, BACK_ORDER = TENSOR, TENSOR
+FINE = (("z", 4), ("yh", 2), ("xh", 2), ("xl", 2), ("yl", 2), ("core", 2))
+DP, TENSOR = ("z", "yh"), ("xh", "xl", "yl", "core")
+OUT_ORDER, BACK_ORDER = ("xl", "xh", "yl", "core"), ("yl", "xl", "xh", "core")
 
 
 def places_of(order):

time: 92.8 us -> 94 us (1.013)
  no operation moved by 1% of the time
where the time goes in v9:
time: 94 us; the launch traced here: 93 us
  blocking collectives  50.9 us (54%)
  Pallas kernels  19.4 us (21%)
  waiting for transfers between devices  16.8 us (18%)
  starting transfers between devices  5.12 us (5%)
    all_to_all x1, blocking collectives, body(): arrived = exchange(outgoing, OUT_ORDER)  32.5 us
    all_to_all x1, blocking collectives, body(): sums = exchange(sums, (DP + TENSOR)[::-1])  18.5 us
    all_to_all x1, waiting for transfers between devices, body(): returned = exchange(step, BACK_ORDER)  16.8 us
    pallas_call x1, Pallas kernels, body(): pl.pallas_call(functools.partial(rest_kernel, out_places, back_places), o...  12.1 us
    all_to_all x1, starting transfers between devices, body(): returned = exchange(step, BACK_ORDER)  5.12 us
    pallas_call x1, Pallas kernels, body(): pl.pallas_call(functools.partial(mid_kernel, out_places), out_shape=(vmem...  2.14 us
    pallas_call x1, Pallas kernels, body(): pl.pallas_call(functools.partial(unpack_kernel, back_places), out_shape=h...  1.96 us
  transfers between devices with their start and end apart: 1, of which 1 were waited for; matrix products, arithmetic and copies ran while one was open for 0% of the time, Pallas kernels for 13%

profile of v9, /device:TPU:9, one launch (start us, length us, event | category | flops | bytes accessed | tf_op | source)
XLA Modules:
  0.0 93.0 jit_solution(10977739315779048621)
XLA Ops:
  0.6 1.6 %pack.1 = f32[16,2,32,512]{3,2,1,0:T(8,128)S(1)} custom-call(s32[1,32]{1,0:T(1,128)} %order_ref.3, f32[512,1024]{1,0:T(8,128)} %grad_ref.1), custom_call_target="tpu_custom_call" | custom-call | tf_op jit(solution)/shard_map/pack/pallas_call | solution.py:246
  2.3 0.0 copy-start
  2.3 0.0 copy-start.2
  2.3 0.0 copy-start.3
  2.3 32.5 %all_to_all.15.arrived_ref = f32[16,2,32,512]{3,2,1,0:T(8,128)S(1)} all-to-all(f32[16,2,32,512]{3,2,1,0:T(8,128)S(1)} %pack.1), channel_id=1, replica_groups=mesh['z'=4,'yh'=2,'xh'=2,'xl'=2,'yl'=2,'core'=2] {'xl','xh','yl','core'}, dimensions={0} | all-to-all | bytes 4194304 | tf_op jit(solution)/shard_map/all_to_all | solution.py:258
  34.7 0.0 copy-done
  34.7 0.0 copy-done.2
  34.7 0.0 copy-done.3
  34.8 0.0 copy-start.1
  34.8 2.1 %mid.1 = (f32[16,2,32,512]{3,2,1,0:T(8,128)S(1)}, f32[16,2,32,512]{3,2,1,0:T(8,128)}, f32[128,2,128]{2,1,0:T(2,128)S(1)}) custom-call(f32[16,2,32,512]{3,2,1,0:T(8,128)S(1)} %all_to_all.15.arrived_ref, f32[2,512,512]{2,1,0:T(8,128)S(1)} %copy-done, bf16[2,512,512]{2,1,0:T(8,128)(2,1)S(1)} %copy-done.2, bf16[2,512,512]{2,1,0:T(8,128)(2,1)S(1)} %copy-done.3), custom_call_target="tpu_custom_call" | custom-call | tf_op jit(solution)/shard_map/mid/pallas_call | solution.py:260
  36.9 18.5 %all_to_all.16.sums_ref = f32[128,2,128]{2,1,0:T(2,128)S(1)} all-to-all(f32[128,2,128]{2,1,0:T(2,128)S(1)} %get-tuple-element.13), channel_id=1, replica_groups=mesh['z'=4,'yh'=2,'xh'=2,'xl'=2,'yl'=2,'core'=2] {'core','yl','xl','xh',..., dimensions={0} | all-to-all | bytes 262144 | tf_op jit(solution)/shard_map/all_to_all | solution.py:269
  55.4 0.0 copy-done.1
  55.4 1.6 %step.1.step_ref = f32[16,2,32,512]{3,2,1,0:T(8,128)} custom-call(f32[128,2,128]{2,1,0:T(2,128)S(1)} %all_to_all.16.sums_ref, f32[16,2,32,512]{3,2,1,0:T(8,128)S(1)} %get-tuple-element.14.shampoo_ref, f32[2,512,512]{2,1,0:T(8,128)S(1)} %copy-done.1), custom_call_target="tpu_custom_call" | custom-call | tf_op jit(solution)/shard_map/step/pallas_call | solution.py:271
  57.0 5.1 %all-to-all-start.2 = ((f32[16,2,32,512]{3,2,1,0:T(8,128)}), f32[16,2,32,512]{3,2,1,0:T(8,128)S(1)}, u32[]{:S(2)}, u32[]{:S(2)}) async-start(f32[16,2,32,512]{3,2,1,0:T(8,128)} %step.1.step_ref), calls=%async_computation.2 | async-start | bytes 4194304 | tf_op jit(solution)/shard_map/all_to_all | solution.py:280
  62.1 12.1 %rest.1 = (f32[2,512,512]{2,1,0:T(8,128)}, f32[2,512,512]{2,1,0:T(8,128)}, f32[2,512,512]{2,1,0:T(8,128)}, f32[2,512,512]{2,1,0:T(8,128)}) custom-call(f32[16,2,32,512]{3,2,1,0:T(8,128)} %get-tuple-element.12.held_ref, f32[2,512,512]{2,1,0:T(8,128)} %second_ref.3, f32[2,512,512]{2,1,0:T(8,128)} %left_ref.3, f32[2,512,512]{2,1,0:T(8,128)} %right_ref.3, ...), custom_call_target="tpu_custom_call" | custom-call | flops 3221225472 | bytes 18874368 | tf_op jit(solution)/shard_map/rest/pallas_call | solution.py:282
  74.3 16.8 %all-to-all-done.2.moved_ref = f32[16,2,32,512]{3,2,1,0:T(8,128)S(1)} async-done(((f32[16,2,32,512]{3,2,1,0:T(8,128)}), f32[16,2,32,512]{3,2,1,0:T(8,128)S(1)}, u32[]{:S(2)}, u32[]{:S(2)}) %all-to-all-start.2) | async-done | bytes 2097184 | tf_op jit(solution)/shard_map/all_to_all | solution.py:280
  91.1 2.0 %unpack.1 = f32[512,1024]{1,0:T(8,128)} custom-call(s32[1,32]{1,0:T(1,128)} %order_ref.3, f32[16,2,32,512]{3,2,1,0:T(8,128)S(1)} %all-to-all-done.2.moved_ref), custom_call_target="tpu_custom_call" | custom-call | tf_op jit(solution)/shard_map/unpack/pallas_call | solution.py:299
Async XLA Ops:
  2.3 32.5 %copy-start = (f32[2,512,512]{2,1,0:T(8,128)S(1)}, f32[2,512,512]{2,1,0:T(8,128)}, u32[]{:S(2)}) copy-start(f32[2,512,512]{2,1,0:T(8,128)} %second_ref.3) | copy-start | bytes 6291460
  2.3 32.5 %copy-start.2 = (bf16[2,512,512]{2,1,0:T(8,128)(2,1)S(1)}, bf16[2,512,512]{2,1,0:T(8,128)(2,1)}, u32[]{:S(2)}) copy-start(bf16[2,512,512]{2,1,0:T(8,128)(2,1)} %left_ref.2) | copy-start | bytes 3145732
  2.3 32.5 %copy-start.3 = (bf16[2,512,512]{2,1,0:T(8,128)(2,1)S(1)}, bf16[2,512,512]{2,1,0:T(8,128)(2,1)}, u32[]{:S(2)}) copy-start(bf16[2,512,512]{2,1,0:T(8,128)(2,1)} %right_ref.2) | copy-start | bytes 3145732
  34.8 20.6 %copy-start.1 = (f32[2,512,512]{2,1,0:T(8,128)S(1)}, f32[2,512,512]{2,1,0:T(8,128)}, u32[]{:S(2)}) copy-start(f32[2,512,512]{2,1,0:T(8,128)} %momentum_ref.3) | copy-start | bytes 6291460
  57.0 34.1 %all-to-all-start.2 = ((f32[16,2,32,512]{3,2,1,0:T(8,128)}), f32[16,2,32,512]{3,2,1,0:T(8,128)S(1)}, u32[]{:S(2)}, u32[]{:S(2)}) async-start(f32[16,2,32,512]{3,2,1,0:T(8,128)} %step.1.step_ref), calls=%async_computation.2 | async-start | bytes 4194304 | tf_op jit(solution)/shard_map/all_to_all | solution.py:280

commit v10 on v8

--- a/solution.py
+++ b/solution.py
@@ -129,7 +129,6 @@
             new_second = 0.99 * second_ref[slot, rows, :] + 0.01 * held * held
             adam = held * pl.reciprocal(jnp.sqrt(new_second) + 1e-08)
             adam_sq += sum_rows(adam * adam)
-    for slot in range(slots):
         applied_ref[slot] = jnp.dot(
             left_ref[slot], low_ref[slot], preferred_element_type=F32
         ).astype(BF16)

time: 92.8 us -> 92.8 us (level)
  no operation moved by 1% of the time
where the time goes in v10:
time: 92.8 us; the launch traced here: 92.6 us
  blocking collectives  50.7 us (55%)
  Pallas kernels  19.4 us (21%)
  waiting for transfers between devices  16.5 us (18%)
  starting transfers between devices  5.17 us (6%)
    all_to_all x1, blocking collectives, body(): arrived = exchange(outgoing, OUT_ORDER)  32.5 us
    all_to_all x1, blocking collectives, body(): sums = exchange(sums, (DP + TENSOR)[::-1])  18.2 us
    all_to_all x1, waiting for transfers between devices, body(): returned = exchange(step, BACK_ORDER)  16.5 us
    pallas_call x1, Pallas kernels, body(): pl.pallas_call(functools.partial(rest_kernel, out_places, back_places), o...  12.1 us
    all_to_all x1, starting transfers between devices, body(): returned = exchange(step, BACK_ORDER)  5.17 us
    pallas_call x1, Pallas kernels, body(): pl.pallas_call(functools.partial(mid_kernel, out_places), out_shape=(vmem...  2.14 us
    pallas_call x1, Pallas kernels, body(): pl.pallas_call(functools.partial(unpack_kernel, back_places), out_shape=h...  1.96 us
  transfers between devices with their start and end apart: 1, of which 1 were waited for; matrix products, arithmetic and copies ran while one was open for 0% of the time, Pallas kernels for 13%

profile of v10, /device:TPU:9, one launch (start us, length us, event | category | flops | bytes accessed | tf_op | source)
XLA Modules:
  0.0 92.6 jit_solution(5208719137134175504)
XLA Ops:
  0.6 1.6 %pack.1 = f32[16,2,32,512]{3,2,1,0:T(8,128)S(1)} custom-call(s32[1,32]{1,0:T(1,128)} %order_ref.3, f32[512,1024]{1,0:T(8,128)} %grad_ref.1), custom_call_target="tpu_custom_call" | custom-call | tf_op jit(solution)/shard_map/pack/pallas_call | solution.py:245
  2.3 0.0 copy-start
  2.3 0.0 copy-start.2
  2.3 0.0 copy-start.3
  2.3 32.5 %all_to_all.15.arrived_ref = f32[16,2,32,512]{3,2,1,0:T(8,128)S(1)} all-to-all(f32[16,2,32,512]{3,2,1,0:T(8,128)S(1)} %pack.1), channel_id=1, replica_groups=mesh['z'=4,'yh'=2,'x'=4,'yl'=2,'core'=2] {'x','yl','core'}, dimensions={0} | all-to-all | bytes 4194304 | tf_op jit(solution)/shard_map/all_to_all | solution.py:257
  34.7 0.0 copy-done
  34.7 0.0 copy-done.2
  34.7 0.0 copy-done.3
  34.8 0.0 copy-start.1
  34.8 2.1 %mid.1 = (f32[16,2,32,512]{3,2,1,0:T(8,128)S(1)}, f32[16,2,32,512]{3,2,1,0:T(8,128)}, f32[128,2,128]{2,1,0:T(2,128)S(1)}) custom-call(f32[16,2,32,512]{3,2,1,0:T(8,128)S(1)} %all_to_all.15.arrived_ref, f32[2,512,512]{2,1,0:T(8,128)S(1)} %copy-done, bf16[2,512,512]{2,1,0:T(8,128)(2,1)S(1)} %copy-done.2, bf16[2,512,512]{2,1,0:T(8,128)(2,1)S(1)} %copy-done.3), custom_call_target="tpu_custom_call" | custom-call | tf_op jit(solution)/shard_map/mid/pallas_call | solution.py:259
  36.9 18.2 %all_to_all.16.sums_ref = f32[128,2,128]{2,1,0:T(2,128)S(1)} all-to-all(f32[128,2,128]{2,1,0:T(2,128)S(1)} %get-tuple-element.13), channel_id=1, replica_groups=mesh['z'=4,'yh'=2,'x'=4,'yl'=2,'core'=2] {'core','yl','x','yh','z'}, dimensions={0} | all-to-all | bytes 262144 | tf_op jit(solution)/shard_map/all_to_all | solution.py:268
  55.2 0.0 copy-done.1
  55.2 1.6 %step.1.step_ref = f32[16,2,32,512]{3,2,1,0:T(8,128)} custom-call(f32[128,2,128]{2,1,0:T(2,128)S(1)} %all_to_all.16.sums_ref, f32[16,2,32,512]{3,2,1,0:T(8,128)S(1)} %get-tuple-element.14.shampoo_ref, f32[2,512,512]{2,1,0:T(8,128)S(1)} %copy-done.1), custom_call_target="tpu_custom_call" | custom-call | tf_op jit(solution)/shard_map/step/pallas_call | solution.py:270
  56.8 5.2 %all-to-all-start.2 = ((f32[16,2,32,512]{3,2,1,0:T(8,128)}), f32[16,2,32,512]{3,2,1,0:T(8,128)S(1)}, u32[]{:S(2)}, u32[]{:S(2)}) async-start(f32[16,2,32,512]{3,2,1,0:T(8,128)} %step.1.step_ref), calls=%async_computation.2 | async-start | bytes 4194304 | tf_op jit(solution)/shard_map/all_to_all | solution.py:279
  61.9 12.1 %rest.1 = (f32[2,512,512]{2,1,0:T(8,128)}, f32[2,512,512]{2,1,0:T(8,128)}, f32[2,512,512]{2,1,0:T(8,128)}, f32[2,512,512]{2,1,0:T(8,128)}) custom-call(f32[16,2,32,512]{3,2,1,0:T(8,128)} %get-tuple-element.12.held_ref, f32[2,512,512]{2,1,0:T(8,128)} %second_ref.3, f32[2,512,512]{2,1,0:T(8,128)} %left_ref.3, f32[2,512,512]{2,1,0:T(8,128)} %right_ref.3, ...), custom_call_target="tpu_custom_call" | custom-call | flops 3221225472 | bytes 18874368 | tf_op jit(solution)/shard_map/rest/pallas_call | solution.py:281
  74.1 16.5 %all-to-all-done.2.moved_ref = f32[16,2,32,512]{3,2,1,0:T(8,128)S(1)} async-done(((f32[16,2,32,512]{3,2,1,0:T(8,128)}), f32[16,2,32,512]{3,2,1,0:T(8,128)S(1)}, u32[]{:S(2)}, u32[]{:S(2)}) %all-to-all-start.2) | async-done | bytes 2097184 | tf_op jit(solution)/shard_map/all_to_all | solution.py:279
  90.6 2.0 %unpack.1 = f32[512,1024]{1,0:T(8,128)} custom-call(s32[1,32]{1,0:T(1,128)} %order_ref.3, f32[16,2,32,512]{3,2,1,0:T(8,128)S(1)} %all-to-all-done.2.moved_ref), custom_call_target="tpu_custom_call" | custom-call | tf_op jit(solution)/shard_map/unpack/pallas_call | solution.py:298
Async XLA Ops:
  2.3 32.5 %copy-start = (f32[2,512,512]{2,1,0:T(8,128)S(1)}, f32[2,512,512]{2,1,0:T(8,128)}, u32[]{:S(2)}) copy-start(f32[2,512,512]{2,1,0:T(8,128)} %second_ref.3) | copy-start | bytes 6291460
  2.3 32.5 %copy-start.2 = (bf16[2,512,512]{2,1,0:T(8,128)(2,1)S(1)}, bf16[2,512,512]{2,1,0:T(8,128)(2,1)}, u32[]{:S(2)}) copy-start(bf16[2,512,512]{2,1,0:T(8,128)(2,1)} %left_ref.2) | copy-start | bytes 3145732
  2.3 32.5 %copy-start.3 = (bf16[2,512,512]{2,1,0:T(8,128)(2,1)S(1)}, bf16[2,512,512]{2,1,0:T(8,128)(2,1)}, u32[]{:S(2)}) copy-start(bf16[2,512,512]{2,1,0:T(8,128)(2,1)} %right_ref.2) | copy-start | bytes 3145732
  34.8 20.4 %copy-start.1 = (f32[2,512,512]{2,1,0:T(8,128)S(1)}, f32[2,512,512]{2,1,0:T(8,128)}, u32[]{:S(2)}) copy-start(f32[2,512,512]{2,1,0:T(8,128)} %momentum_ref.3) | copy-start | bytes 6291460
  56.8 33.8 %all-to-all-start.2 = ((f32[16,2,32,512]{3,2,1,0:T(8,128)}), f32[16,2,32,512]{3,2,1,0:T(8,128)S(1)}, u32[]{:S(2)}, u32[]{:S(2)}) async-start(f32[16,2,32,512]{3,2,1,0:T(8,128)} %step.1.step_ref), calls=%async_computation.2 | async-start | bytes 4194304 | tf_op jit(solution)/shard_map/all_to_all | solution.py:279

commit v11 on v8

--- a/solution.py
+++ b/solution.py
@@ -72,7 +72,7 @@
 
 
 def pack_kernel(
-    places, order_ref, grad_ref, out_ref, here_ref, order_here, index_ref, sems, order_sem
+    places, order_ref, grad_ref, out_ref, order_here, here_ref, index_ref, sems, order_sem
 ):
     peers, slots, piece_rows, block_size = out_ref.shape
     table = started(order_ref, order_here, order_sem)
@@ -243,14 +243,13 @@
     exchange = functools.partial(lax.all_to_all, split_axis=0, concat_axis=0, tiled=True)
     order = in_hbm(owner_order)
 
-    outgoing = pl.pallas_call(
+    outgoing, table = pl.pallas_call(
         functools.partial(pack_kernel, out_places),
-        out_shape=vmem(pair),
+        out_shape=(vmem(pair), pltpu.SMEM(owner_order.shape, jnp.int32)),
         in_specs=[ANY, ANY],
-        out_specs=VMEM,
+        out_specs=(VMEM, pl.BlockSpec(memory_space=pltpu.SMEM)),
         scratch_shapes=[
-            vmem(grad.shape), pltpu.SMEM(owner_order.shape, jnp.int32),
-            pltpu.SMEM((peers * slots,), jnp.int32), DMA((2 * CHUNKS,)), DMA,
+            vmem(grad.shape), pltpu.SMEM((peers * slots,), jnp.int32), DMA((2 * CHUNKS,)), DMA,
         ],
         compiler_params=params(8),
         name="pack",
@@ -304,7 +303,7 @@
         scratch_shapes=[DMA],
         compiler_params=params(8),
         name="unpack",
-    )(order, in_vmem(returned))
+    )(table, in_vmem(returned))
     return (new_left, new_right, new_momentum, new_second, update)
 
 

time: 92.8 us -> 92.1 us (level)
  no operation moved by 1% of the time
where the time goes in v11:
time: 92.1 us; the launch traced here: 91.9 us
  blocking collectives  50.7 us (55%)
  Pallas kernels  18.8 us (20%)
  waiting for transfers between devices  16.5 us (18%)
  starting transfers between devices  5.17 us (6%)
    all_to_all x1, blocking collectives, body(): arrived = exchange(outgoing, OUT_ORDER)  32.5 us
    all_to_all x1, blocking collectives, body(): sums = exchange(sums, (DP + TENSOR)[::-1])  18.2 us
    all_to_all x1, waiting for transfers between devices, body(): returned = exchange(step, BACK_ORDER)  16.5 us
    pallas_call x1, Pallas kernels, body(): pl.pallas_call(functools.partial(rest_kernel, out_places, back_places), o...  12.1 us
    all_to_all x1, starting transfers between devices, body(): returned = exchange(step, BACK_ORDER)  5.17 us
    pallas_call x1, Pallas kernels, body(): pl.pallas_call(functools.partial(mid_kernel, out_places), out_shape=(vmem...  2.15 us
  transfers between devices with their start and end apart: 1, of which 1 were waited for; matrix products, arithmetic and copies ran while one was open for 0% of the time, Pallas kernels for 13%

profile of v11, /device:TPU:9, one launch (start us, length us, event | category | flops | bytes accessed | tf_op | source)
XLA Modules:
  0.0 91.9 jit_solution(6683690002529819598)
XLA Ops:
  0.6 1.6 %pack.1 = (f32[16,2,32,512]{3,2,1,0:T(8,128)S(1)}, s32[1,32]{1,0:T(1,128)S(4)}) custom-call(s32[1,32]{1,0:T(1,128)} %order_ref.1, f32[512,1024]{1,0:T(8,128)} %grad_ref.1), custom_call_target="tpu_custom_call" | custom-call | tf_op jit(solution)/shard_map/pack/pallas_call | solution.py:246
  2.3 0.0 copy-start
  2.3 0.0 copy-start.2
  2.3 0.0 copy-start.3
  2.3 32.5 %all_to_all.15.arrived_ref = f32[16,2,32,512]{3,2,1,0:T(8,128)S(1)} all-to-all(f32[16,2,32,512]{3,2,1,0:T(8,128)S(1)} %get-tuple-element.14), channel_id=1, replica_groups=mesh['z'=4,'yh'=2,'x'=4,'yl'=2,'core'=2] {'x','yl','core'}, dimensions={0} | all-to-all | bytes 4194304 | tf_op jit(solution)/shard_map/all_to_all | solution.py:257
  34.7 0.0 copy-done
  34.7 0.0 copy-done.2
  34.7 0.0 copy-done.3
  34.8 0.0 copy-start.1
  34.8 2.1 %mid.1 = (f32[16,2,32,512]{3,2,1,0:T(8,128)S(1)}, f32[16,2,32,512]{3,2,1,0:T(8,128)}, f32[128,2,128]{2,1,0:T(2,128)S(1)}) custom-call(f32[16,2,32,512]{3,2,1,0:T(8,128)S(1)} %all_to_all.15.arrived_ref, f32[2,512,512]{2,1,0:T(8,128)S(1)} %copy-done, bf16[2,512,512]{2,1,0:T(8,128)(2,1)S(1)} %copy-done.2, bf16[2,512,512]{2,1,0:T(8,128)(2,1)S(1)} %copy-done.3), custom_call_target="tpu_custom_call" | custom-call | tf_op jit(solution)/shard_map/mid/pallas_call | solution.py:259
  36.9 18.2 %all_to_all.16.sums_ref = f32[128,2,128]{2,1,0:T(2,128)S(1)} all-to-all(f32[128,2,128]{2,1,0:T(2,128)S(1)} %get-tuple-element.16), channel_id=1, replica_groups=mesh['z'=4,'yh'=2,'x'=4,'yl'=2,'core'=2] {'core','yl','x','yh','z'}, dimensions={0} | all-to-all | bytes 262144 | tf_op jit(solution)/shard_map/all_to_all | solution.py:268
  55.2 0.0 copy-done.1
  55.2 1.6 %step.1.step_ref = f32[16,2,32,512]{3,2,1,0:T(8,128)} custom-call(f32[128,2,128]{2,1,0:T(2,128)S(1)} %all_to_all.16.sums_ref, f32[16,2,32,512]{3,2,1,0:T(8,128)S(1)} %get-tuple-element.17.shampoo_ref, f32[2,512,512]{2,1,0:T(8,128)S(1)} %copy-done.1), custom_call_target="tpu_custom_call" | custom-call | tf_op jit(solution)/shard_map/step/pallas_call | solution.py:270
  56.8 5.2 %all-to-all-start.2 = ((f32[16,2,32,512]{3,2,1,0:T(8,128)}), f32[16,2,32,512]{3,2,1,0:T(8,128)S(1)}, u32[]{:S(2)}, u32[]{:S(2)}) async-start(f32[16,2,32,512]{3,2,1,0:T(8,128)} %step.1.step_ref), calls=%async_computation.2 | async-start | bytes 4194304 | tf_op jit(solution)/shard_map/all_to_all | solution.py:279
  61.9 12.1 %rest.1 = (f32[2,512,512]{2,1,0:T(8,128)}, f32[2,512,512]{2,1,0:T(8,128)}, f32[2,512,512]{2,1,0:T(8,128)}, f32[2,512,512]{2,1,0:T(8,128)}) custom-call(f32[16,2,32,512]{3,2,1,0:T(8,128)} %get-tuple-element.15.held_ref, f32[2,512,512]{2,1,0:T(8,128)} %second_ref.3, f32[2,512,512]{2,1,0:T(8,128)} %left_ref.3, f32[2,512,512]{2,1,0:T(8,128)} %right_ref.3, ...), custom_call_target="tpu_custom_call" | custom-call | flops 3221225472 | bytes 18874368 | tf_op jit(solution)/shard_map/rest/pallas_call | solution.py:281
  74.1 16.5 %all-to-all-done.2.moved_ref = f32[16,2,32,512]{3,2,1,0:T(8,128)S(1)} async-done(((f32[16,2,32,512]{3,2,1,0:T(8,128)}), f32[16,2,32,512]{3,2,1,0:T(8,128)S(1)}, u32[]{:S(2)}, u32[]{:S(2)}) %all-to-all-start.2) | async-done | bytes 2097184 | tf_op jit(solution)/shard_map/all_to_all | solution.py:279
  90.6 1.3 %unpack.1 = f32[512,1024]{1,0:T(8,128)} custom-call(s32[1,32]{1,0:T(1,128)S(4)} %get-tuple-element.22.order_ref, f32[16,2,32,512]{3,2,1,0:T(8,128)S(1)} %all-to-all-done.2.moved_ref), custom_call_target="tpu_custom_call" | custom-call | tf_op jit(solution)/shard_map/unpack/pallas_call | solution.py:298
Async XLA Ops:
  2.3 32.5 %copy-start = (f32[2,512,512]{2,1,0:T(8,128)S(1)}, f32[2,512,512]{2,1,0:T(8,128)}, u32[]{:S(2)}) copy-start(f32[2,512,512]{2,1,0:T(8,128)} %second_ref.3) | copy-start | bytes 6291460
  2.3 32.5 %copy-start.2 = (bf16[2,512,512]{2,1,0:T(8,128)(2,1)S(1)}, bf16[2,512,512]{2,1,0:T(8,128)(2,1)}, u32[]{:S(2)}) copy-start(bf16[2,512,512]{2,1,0:T(8,128)(2,1)} %left_ref.2) | copy-start | bytes 3145732
  2.3 32.5 %copy-start.3 = (bf16[2,512,512]{2,1,0:T(8,128)(2,1)S(1)}, bf16[2,512,512]{2,1,0:T(8,128)(2,1)}, u32[]{:S(2)}) copy-start(bf16[2,512,512]{2,1,0:T(8,128)(2,1)} %right_ref.2) | copy-start | bytes 3145732
  34.8 20.4 %copy-start.1 = (f32[2,512,512]{2,1,0:T(8,128)S(1)}, f32[2,512,512]{2,1,0:T(8,128)}, u32[]{:S(2)}) copy-start(f32[2,512,512]{2,1,0:T(8,128)} %momentum_ref.3) | copy-start | bytes 6291460
  56.8 33.8 %all-to-all-start.2 = ((f32[16,2,32,512]{3,2,1,0:T(8,128)}), f32[16,2,32,512]{3,2,1,0:T(8,128)S(1)}, u32[]{:S(2)}, u32[]{:S(2)}) async-start(f32[16,2,32,512]{3,2,1,0:T(8,128)} %step.1.step_ref), calls=%async_computation.2 | async-start | bytes 4194304 | tf_op jit(solution)/shard_map/all_to_all | solution.py:279

commit v12 on v11

--- a/solution.py
+++ b/solution.py
@@ -137,7 +137,7 @@
         shampoo = jnp.dot(applied_ref[slot], right_ref[slot], preferred_element_type=F32)
         shampoo_ref[:, slot] = shampoo.reshape(peers, piece_rows, block_size)
         shampoo_sq += sum_rows(shampoo * shampoo)
-    first = lax.broadcasted_iota(jnp.int32, (2, 128), 0) == 0
+    first = lax.broadcasted_iota(jnp.int32, (1, 128), 1) < 64
     sums = jnp.where(first, jnp.sum(adam_sq), jnp.sum(shampoo_sq))
     sums_ref[...] = jnp.broadcast_to(sums[None], sums_ref.shape)
     kept.wait()
@@ -145,13 +145,13 @@
 
 def graft_of(sums_ref):
     root = jnp.sqrt(jnp.sum(sums_ref[...], axis=0))
-    return root[0:1, 0:1] / (root[1:2, 0:1] + 1e-06)
+    return root[0:1, 0:1] / (root[0:1, 64:65] + 1e-06)
 
 
 def step_kernel(places, sums_ref, shampoo_ref, momentum_ref, step_ref, here_ref, sem):
     peers, slots, piece_rows, block_size = shampoo_ref.shape
     graft = graft_of(sums_ref)
-    count = peers // (2 * CHUNKS)
+    count = peers // (4 * CHUNKS)
     for peer in range(peers):
         rows = rows_of(places[peer], piece_rows)
         for slot in range(slots):
@@ -258,7 +258,7 @@
 
     shampoo, held, sums = pl.pallas_call(
         functools.partial(mid_kernel, out_places),
-        out_shape=(vmem(pair), hbm(pair), jax.ShapeDtypeStruct((ranks, 2, 128), F32)),
+        out_shape=(vmem(pair), hbm(pair), jax.ShapeDtypeStruct((ranks, 1, 128), F32)),
         in_specs=[VMEM] * 4,
         out_specs=(VMEM, ANY, VMEM),
         scratch_shapes=[vmem(blocks, BF16), vmem(blocks, BF16), DMA],

time: 92.1 us -> 91.8 us (level)
  no operation moved by 1% of the time
where the time goes in v12:
time: 91.8 us; the launch traced here: 91.6 us
  blocking collectives  50.3 us (55%)
  Pallas kernels  18.8 us (20%)
  waiting for transfers between devices  16.5 us (18%)
  starting transfers between devices  5.18 us (6%)
    all_to_all x1, blocking collectives, body(): arrived = exchange(outgoing, OUT_ORDER)  32.5 us
    all_to_all x1, blocking collectives, body(): sums = exchange(sums, (DP + TENSOR)[::-1])  17.9 us
    all_to_all x1, waiting for transfers between devices, body(): returned = exchange(step, BACK_ORDER)  16.5 us
    pallas_call x1, Pallas kernels, body(): pl.pallas_call(functools.partial(rest_kernel, out_places, back_places), o...  12.1 us
    all_to_all x1, starting transfers between devices, body(): returned = exchange(step, BACK_ORDER)  5.18 us
    pallas_call x1, Pallas kernels, body(): pl.pallas_call(functools.partial(mid_kernel, out_places), out_shape=(vmem...  2.15 us
  transfers between devices with their start and end apart: 1, of which 1 were waited for; matrix products, arithmetic and copies ran while one was open for 0% of the time, Pallas kernels for 13%

profile of v12, /device:TPU:9, one launch (start us, length us, event | category | flops | bytes accessed | tf_op | source)
XLA Modules:
  0.0 91.6 jit_solution(8068654008695988172)
XLA Ops:
  0.6 1.6 %pack.1 = (f32[16,2,32,512]{3,2,1,0:T(8,128)S(1)}, s32[1,32]{1,0:T(1,128)S(4)}) custom-call(s32[1,32]{1,0:T(1,128)} %order_ref.1, f32[512,1024]{1,0:T(8,128)} %grad_ref.1), custom_call_target="tpu_custom_call" | custom-call | tf_op jit(solution)/shard_map/pack/pallas_call | solution.py:246
  2.3 0.0 copy-start
  2.3 0.0 copy-start.2
  2.3 0.0 copy-start.3
  2.3 32.5 %all_to_all.15.arrived_ref = f32[16,2,32,512]{3,2,1,0:T(8,128)S(1)} all-to-all(f32[16,2,32,512]{3,2,1,0:T(8,128)S(1)} %get-tuple-element.14), channel_id=1, replica_groups=mesh['z'=4,'yh'=2,'x'=4,'yl'=2,'core'=2] {'x','yl','core'}, dimensions={0} | all-to-all | bytes 4194304 | tf_op jit(solution)/shard_map/all_to_all | solution.py:257
  34.7 0.0 copy-done
  34.7 0.0 copy-done.2
  34.7 0.0 copy-done.3
  34.8 0.0 copy-start.1
  34.8 2.1 %mid.1 = (f32[16,2,32,512]{3,2,1,0:T(8,128)S(1)}, f32[16,2,32,512]{3,2,1,0:T(8,128)}, f32[128,1,128]{2,1,0:T(1,128)S(1)}) custom-call(f32[16,2,32,512]{3,2,1,0:T(8,128)S(1)} %all_to_all.15.arrived_ref, f32[2,512,512]{2,1,0:T(8,128)S(1)} %copy-done, bf16[2,512,512]{2,1,0:T(8,128)(2,1)S(1)} %copy-done.2, bf16[2,512,512]{2,1,0:T(8,128)(2,1)S(1)} %copy-done.3), custom_call_target="tpu_custom_call" | custom-call | tf_op jit(solution)/shard_map/mid/pallas_call | solution.py:259
  36.9 17.9 %all_to_all.16.sums_ref = f32[128,1,128]{2,1,0:T(1,128)S(1)} all-to-all(f32[128,1,128]{2,1,0:T(1,128)S(1)} %get-tuple-element.16), channel_id=1, replica_groups=mesh['z'=4,'yh'=2,'x'=4,'yl'=2,'core'=2] {'core','yl','x','yh','z'}, dimensions={0} | all-to-all | bytes 131072 | tf_op jit(solution)/shard_map/all_to_all | solution.py:268
  54.8 0.0 copy-done.1
  54.8 1.6 %step.1.step_ref = f32[16,2,32,512]{3,2,1,0:T(8,128)} custom-call(f32[128,1,128]{2,1,0:T(1,128)S(1)} %all_to_all.16.sums_ref, f32[16,2,32,512]{3,2,1,0:T(8,128)S(1)} %get-tuple-element.17.shampoo_ref, f32[2,512,512]{2,1,0:T(8,128)S(1)} %copy-done.1), custom_call_target="tpu_custom_call" | custom-call | tf_op jit(solution)/shard_map/step/pallas_call | solution.py:270
  56.4 5.2 %all-to-all-start.2 = ((f32[16,2,32,512]{3,2,1,0:T(8,128)}), f32[16,2,32,512]{3,2,1,0:T(8,128)S(1)}, u32[]{:S(2)}, u32[]{:S(2)}) async-start(f32[16,2,32,512]{3,2,1,0:T(8,128)} %step.1.step_ref), calls=%async_computation.2 | async-start | bytes 4194304 | tf_op jit(solution)/shard_map/all_to_all | solution.py:279
  61.6 12.1 %rest.1 = (f32[2,512,512]{2,1,0:T(8,128)}, f32[2,512,512]{2,1,0:T(8,128)}, f32[2,512,512]{2,1,0:T(8,128)}, f32[2,512,512]{2,1,0:T(8,128)}) custom-call(f32[16,2,32,512]{3,2,1,0:T(8,128)} %get-tuple-element.15.held_ref, f32[2,512,512]{2,1,0:T(8,128)} %second_ref.3, f32[2,512,512]{2,1,0:T(8,128)} %left_ref.3, f32[2,512,512]{2,1,0:T(8,128)} %right_ref.3, ...), custom_call_target="tpu_custom_call" | custom-call | flops 3221225472 | bytes 18874368 | tf_op jit(solution)/shard_map/rest/pallas_call | solution.py:281
  73.7 16.5 %all-to-all-done.2.moved_ref = f32[16,2,32,512]{3,2,1,0:T(8,128)S(1)} async-done(((f32[16,2,32,512]{3,2,1,0:T(8,128)}), f32[16,2,32,512]{3,2,1,0:T(8,128)S(1)}, u32[]{:S(2)}, u32[]{:S(2)}) %all-to-all-start.2) | async-done | bytes 2097184 | tf_op jit(solution)/shard_map/all_to_all | solution.py:279
  90.3 1.3 %unpack.1 = f32[512,1024]{1,0:T(8,128)} custom-call(s32[1,32]{1,0:T(1,128)S(4)} %get-tuple-element.22.order_ref, f32[16,2,32,512]{3,2,1,0:T(8,128)S(1)} %all-to-all-done.2.moved_ref), custom_call_target="tpu_custom_call" | custom-call | tf_op jit(solution)/shard_map/unpack/pallas_call | solution.py:298
Async XLA Ops:
  2.3 32.5 %copy-start = (f32[2,512,512]{2,1,0:T(8,128)S(1)}, f32[2,512,512]{2,1,0:T(8,128)}, u32[]{:S(2)}) copy-start(f32[2,512,512]{2,1,0:T(8,128)} %second_ref.3) | copy-start | bytes 6291460
  2.3 32.5 %copy-start.2 = (bf16[2,512,512]{2,1,0:T(8,128)(2,1)S(1)}, bf16[2,512,512]{2,1,0:T(8,128)(2,1)}, u32[]{:S(2)}) copy-start(bf16[2,512,512]{2,1,0:T(8,128)(2,1)} %left_ref.2) | copy-start | bytes 3145732
  2.3 32.5 %copy-start.3 = (bf16[2,512,512]{2,1,0:T(8,128)(2,1)S(1)}, bf16[2,512,512]{2,1,0:T(8,128)(2,1)}, u32[]{:S(2)}) copy-start(bf16[2,512,512]{2,1,0:T(8,128)(2,1)} %right_ref.2) | copy-start | bytes 3145732
  34.8 20.0 %copy-start.1 = (f32[2,512,512]{2,1,0:T(8,128)S(1)}, f32[2,512,512]{2,1,0:T(8,128)}, u32[]{:S(2)}) copy-start(f32[2,512,512]{2,1,0:T(8,128)} %momentum_ref.3) | copy-start | bytes 6291460
  56.4 33.9 %all-to-all-start.2 = ((f32[16,2,32,512]{3,2,1,0:T(8,128)}), f32[16,2,32,512]{3,2,1,0:T(8,128)S(1)}, u32[]{:S(2)}, u32[]{:S(2)}) async-start(f32[16,2,32,512]{3,2,1,0:T(8,128)} %step.1.step_ref), calls=%async_computation.2 | async-start | bytes 4194304 | tf_op jit(solution)/shard_map/all_to_all | solution.py:279

commit v13 on v12

--- a/solution.py
+++ b/solution.py
@@ -151,7 +151,7 @@
 def step_kernel(places, sums_ref, shampoo_ref, momentum_ref, step_ref, here_ref, sem):
     peers, slots, piece_rows, block_size = shampoo_ref.shape
     graft = graft_of(sums_ref)
-    count = peers // (4 * CHUNKS)
+    count = peers // (2 * CHUNKS)
     for peer in range(peers):
         rows = rows_of(places[peer], piece_rows)
         for slot in range(slots):
@@ -249,7 +249,7 @@
         in_specs=[ANY, ANY],
         out_specs=(VMEM, pl.BlockSpec(memory_space=pltpu.SMEM)),
         scratch_shapes=[
-            vmem(grad.shape), pltpu.SMEM((peers * slots,), jnp.int32), DMA((2 * CHUNKS,)), DMA,
+            vmem(grad.shape), pltpu.SMEM((peers * slots,), jnp.int32), DMA((4 * CHUNKS,)), DMA,
         ],
         compiler_params=params(8),
         name="pack",

time: 91.8 us -> 92 us (level)
  no operation moved by 1% of the time
where the time goes in v13:
time: 92 us; the launch traced here: 91.8 us
  blocking collectives  50.3 us (55%)
  Pallas kernels  19 us (21%)
  waiting for transfers between devices  16.5 us (18%)
  starting transfers between devices  5.18 us (6%)
    all_to_all x1, blocking collectives, body(): arrived = exchange(outgoing, OUT_ORDER)  32.5 us
    all_to_all x1, blocking collectives, body(): sums = exchange(sums, (DP + TENSOR)[::-1])  17.9 us
    all_to_all x1, waiting for transfers between devices, body(): returned = exchange(step, BACK_ORDER)  16.5 us
    pallas_call x1, Pallas kernels, body(): pl.pallas_call(functools.partial(rest_kernel, out_places, back_places), o...  12.1 us
    all_to_all x1, starting transfers between devices, body(): returned = exchange(step, BACK_ORDER)  5.18 us
    pallas_call x1, Pallas kernels, body(): pl.pallas_call(functools.partial(mid_kernel, out_places), out_shape=(vmem...  2.14 us
  transfers between devices with their start and end apart: 1, of which 1 were waited for; matrix products, arithmetic and copies ran while one was open for 0% of the time, Pallas kernels for 13%

profile of v13, /device:TPU:9, one launch (start us, length us, event | category | flops | bytes accessed | tf_op | source)
XLA Modules:
  0.0 91.8 jit_solution(13010428478019710033)
XLA Ops:
  0.6 1.8 %pack.1 = (f32[16,2,32,512]{3,2,1,0:T(8,128)S(1)}, s32[1,32]{1,0:T(1,128)S(4)}) custom-call(s32[1,32]{1,0:T(1,128)} %order_ref.1, f32[512,1024]{1,0:T(8,128)} %grad_ref.1), custom_call_target="tpu_custom_call" | custom-call | tf_op jit(solution)/shard_map/pack/pallas_call | solution.py:246
  2.4 0.0 copy-start
  2.4 0.0 copy-start.2
  2.4 0.0 copy-start.3
  2.4 32.5 %all_to_all.15.arrived_ref = f32[16,2,32,512]{3,2,1,0:T(8,128)S(1)} all-to-all(f32[16,2,32,512]{3,2,1,0:T(8,128)S(1)} %get-tuple-element.14), channel_id=1, replica_groups=mesh['z'=4,'yh'=2,'x'=4,'yl'=2,'core'=2] {'x','yl','core'}, dimensions={0} | all-to-all | bytes 4194304 | tf_op jit(solution)/shard_map/all_to_all | solution.py:257
  34.9 0.0 copy-done
  34.9 0.0 copy-done.2
  34.9 0.0 copy-done.3
  34.9 0.0 copy-start.1
  34.9 2.1 %mid.1 = (f32[16,2,32,512]{3,2,1,0:T(8,128)S(1)}, f32[16,2,32,512]{3,2,1,0:T(8,128)}, f32[128,1,128]{2,1,0:T(1,128)S(1)}) custom-call(f32[16,2,32,512]{3,2,1,0:T(8,128)S(1)} %all_to_all.15.arrived_ref, f32[2,512,512]{2,1,0:T(8,128)S(1)} %copy-done, bf16[2,512,512]{2,1,0:T(8,128)(2,1)S(1)} %copy-done.2, bf16[2,512,512]{2,1,0:T(8,128)(2,1)S(1)} %copy-done.3), custom_call_target="tpu_custom_call" | custom-call | tf_op jit(solution)/shard_map/mid/pallas_call | solution.py:259
  37.1 17.9 %all_to_all.16.sums_ref = f32[128,1,128]{2,1,0:T(1,128)S(1)} all-to-all(f32[128,1,128]{2,1,0:T(1,128)S(1)} %get-tuple-element.16), channel_id=1, replica_groups=mesh['z'=4,'yh'=2,'x'=4,'yl'=2,'core'=2] {'core','yl','x','yh','z'}, dimensions={0} | all-to-all | bytes 131072 | tf_op jit(solution)/shard_map/all_to_all | solution.py:268
  54.9 0.0 copy-done.1
  54.9 1.7 %step.1.step_ref = f32[16,2,32,512]{3,2,1,0:T(8,128)} custom-call(f32[128,1,128]{2,1,0:T(1,128)S(1)} %all_to_all.16.sums_ref, f32[16,2,32,512]{3,2,1,0:T(8,128)S(1)} %get-tuple-element.17.shampoo_ref, f32[2,512,512]{2,1,0:T(8,128)S(1)} %copy-done.1), custom_call_target="tpu_custom_call" | custom-call | tf_op jit(solution)/shard_map/step/pallas_call | solution.py:270
  56.6 5.2 %all-to-all-start.2 = ((f32[16,2,32,512]{3,2,1,0:T(8,128)}), f32[16,2,32,512]{3,2,1,0:T(8,128)S(1)}, u32[]{:S(2)}, u32[]{:S(2)}) async-start(f32[16,2,32,512]{3,2,1,0:T(8,128)} %step.1.step_ref), calls=%async_computation.2 | async-start | bytes 4194304 | tf_op jit(solution)/shard_map/all_to_all | solution.py:279
  61.8 12.1 %rest.1 = (f32[2,512,512]{2,1,0:T(8,128)}, f32[2,512,512]{2,1,0:T(8,128)}, f32[2,512,512]{2,1,0:T(8,128)}, f32[2,512,512]{2,1,0:T(8,128)}) custom-call(f32[16,2,32,512]{3,2,1,0:T(8,128)} %get-tuple-element.15.held_ref, f32[2,512,512]{2,1,0:T(8,128)} %second_ref.3, f32[2,512,512]{2,1,0:T(8,128)} %left_ref.3, f32[2,512,512]{2,1,0:T(8,128)} %right_ref.3, ...), custom_call_target="tpu_custom_call" | custom-call | flops 3221225472 | bytes 18874368 | tf_op jit(solution)/shard_map/rest/pallas_call | solution.py:281
  73.9 16.5 %all-to-all-done.2.moved_ref = f32[16,2,32,512]{3,2,1,0:T(8,128)S(1)} async-done(((f32[16,2,32,512]{3,2,1,0:T(8,128)}), f32[16,2,32,512]{3,2,1,0:T(8,128)S(1)}, u32[]{:S(2)}, u32[]{:S(2)}) %all-to-all-start.2) | async-done | bytes 2097184 | tf_op jit(solution)/shard_map/all_to_all | solution.py:279
  90.5 1.3 %unpack.1 = f32[512,1024]{1,0:T(8,128)} custom-call(s32[1,32]{1,0:T(1,128)S(4)} %get-tuple-element.22.order_ref, f32[16,2,32,512]{3,2,1,0:T(8,128)S(1)} %all-to-all-done.2.moved_ref), custom_call_target="tpu_custom_call" | custom-call | tf_op jit(solution)/shard_map/unpack/pallas_call | solution.py:298
Async XLA Ops:
  2.4 32.5 %copy-start = (f32[2,512,512]{2,1,0:T(8,128)S(1)}, f32[2,512,512]{2,1,0:T(8,128)}, u32[]{:S(2)}) copy-start(f32[2,512,512]{2,1,0:T(8,128)} %second_ref.3) | copy-start | bytes 6291460
  2.4 32.5 %copy-start.2 = (bf16[2,512,512]{2,1,0:T(8,128)(2,1)S(1)}, bf16[2,512,512]{2,1,0:T(8,128)(2,1)}, u32[]{:S(2)}) copy-start(bf16[2,512,512]{2,1,0:T(8,128)(2,1)} %left_ref.2) | copy-start | bytes 3145732
  2.4 32.5 %copy-start.3 = (bf16[2,512,512]{2,1,0:T(8,128)(2,1)S(1)}, bf16[2,512,512]{2,1,0:T(8,128)(2,1)}, u32[]{:S(2)}) copy-start(bf16[2,512,512]{2,1,0:T(8,128)(2,1)} %right_ref.2) | copy-start | bytes 3145732
  34.9 20.0 %copy-start.1 = (f32[2,512,512]{2,1,0:T(8,128)S(1)}, f32[2,512,512]{2,1,0:T(8,128)}, u32[]{:S(2)}) copy-start(f32[2,512,512]{2,1,0:T(8,128)} %momentum_ref.3) | copy-start | bytes 6291460
  56.6 33.9 %all-to-all-start.2 = ((f32[16,2,32,512]{3,2,1,0:T(8,128)}), f32[16,2,32,512]{3,2,1,0:T(8,128)S(1)}, u32[]{:S(2)}, u32[]{:S(2)}) async-start(f32[16,2,32,512]{3,2,1,0:T(8,128)} %step.1.step_ref), calls=%async_computation.2 | async-start | bytes 4194304 | tf_op jit(solution)/shard_map/all_to_all | solution.py:279
